TPU v7x, 512 devices: a whole 4x4x16 slice. The times are simulated.
512 devices in a mesh: tile: 32 (over z, x_lo), mode: 16 (over y, x_hi, core).
Axes of the slice: x: 4 (x_hi: 2, x_lo: 2; x = x_hi * 2 + x_lo), y: 4, z: 16, core: 2. Of those that a mesh axis runs over, the one named last changes fastest.
Arguments:
- charges: bfloat16 [512, 2, 32768], P('mode', None, 'tile'), may hold values from -6 to 6
- proxy: bfloat16 [512, 256, 128], P('mode'), may hold values from -0.5 to 0.5
- tile_boxes: int32 [4096, 4], P('tile'), may hold values from 0 to 1023, as said below
- box_skel: int32 [1024, 32], replicated, may hold values from 0 to 32767, as said below
Outputs:
- potential: bfloat16 [256, 4096, 1024], P('mode', 'tile')
Inputs may be any that keep to these rules, and one draw needn't show every extreme that they name: `tile_boxes`: every box named for a tile of rows [i * 128, (i + 1) * 128) belongs to an index within 1 of i, box b belonging to index b // 32. `box_skel`: the indices of one box are distinct and lie in [o * 1024, (o + 1) * 1024) with o = b // 32; no two boxes share an index.
All inputs are finite; a program needn't handle non-finite values.
Results may differ from a plain program's by a relative error of at most 0.0055.
Values may be sent and summed in bfloat16 or wider, within the bound.
No kernel may reach another device: no remote copies, remote signals or barrier semaphores. Data moves between devices by JAX's collectives and lax.ppermute only.
A program may use at most 64 MiB of HBM per device.

v0:
```python
import math

import jax
import jax.numpy as jnp
from jax import lax
from jax.sharding import PartitionSpec as P


def extended(array, sides, width):
    for axis, dim in sides:
        peers, length = (lax.axis_size(axis), array.shape[dim])
        up = [(i, (i + 1) % peers) for i in range(peers - 1)]
        down = [(j, i) for i, j in up]
        last = lax.slice_in_dim(array, length - width, length, axis=dim)
        first = lax.slice_in_dim(array, 0, width, axis=dim)
        before = lax.ppermute(last, axis, up)
        after = lax.ppermute(first, axis, down)
        array = jnp.concatenate([before, array, after], axis=dim)
    return array


def synthesis_table(modes):
    angles = 2 * modes
    order = jnp.arange(modes, dtype=jnp.int32)
    angle_ids = jnp.arange(angles, dtype=jnp.int32)
    phase = (order[:, None] * angle_ids[None, :] % angles).astype(jnp.float32) * (
        2.0 * math.pi / angles
    )
    weight = jnp.where(order == 0, 1.0, 2.0).astype(jnp.float32) / math.sqrt(2.0 * modes)
    table = jnp.stack([weight[:, None] * jnp.cos(phase), -weight[:, None] * jnp.sin(phase)], axis=1)
    return table.reshape(2 * modes, angles).astype(jnp.bfloat16)


def shards(charges, proxy, tile_boxes, box_skel):
    modes_here, parts, skel_here = charges.shape
    tiles_here, list_len = tile_boxes.shape
    listed = jnp.take(box_skel, tile_boxes.reshape(-1), axis=0).reshape(tiles_here, -1)
    source = extended(charges, (("tile", 2),), skel_here)
    local_ids = listed - (lax.axis_index("tile") - 1) * skel_here
    flat_source = source.reshape(modes_here * parts, -1)
    picked = jnp.take(flat_source, local_ids.reshape(-1), axis=1)
    picked = picked.reshape(modes_here, parts, tiles_here, -1)
    wide_proxy = jnp.broadcast_to(proxy[:, None], (modes_here, parts) + proxy.shape[1:])
    field = lax.dot_general(
        wide_proxy, picked, (((3,), (3,)), ((0, 1), (0, 1))), preferred_element_type=jnp.float32
    )
    field = field.astype(jnp.bfloat16)
    modes_all = modes_here * lax.axis_size("mode")
    table = synthesis_table(modes_all)
    block = lax.all_to_all(field, "mode", split_axis=2, concat_axis=0, tiled=True)
    width = block.shape[2]
    count = block.shape[3]
    flat = block.reshape(2 * modes_all, width * count)
    result = lax.dot_general(
        flat, table, (((0,), (0,)), ((), ())), preferred_element_type=jnp.float32
    )
    return result.reshape(width, count, -1).astype(jnp.bfloat16)


def solution(mesh):
    placed = (P("mode", None, "tile"), P("mode", None, None), P("tile", None), P())
    return jax.shard_map(
        shards, mesh=mesh, in_specs=placed, out_specs=P("mode", "tile", None), check_vma=False
    )
```

profile of v0, /device:TPU:1, one launch (start us, length us, event | category | flops | bytes accessed | tf_op | source)
XLA Modules:
  0.0 179.2 jit_solution(6958424008232963945)
XLA Ops:
  0.0 0.0 copy-start
  0.0 4.1 %collective-permute-start = (bf16[32,2,1024]{2,1,0:T(2,128)(2,1)}, bf16[32,2,1024]{2,1,0:T(2,128)(2,1)S(1)}, u32[]{:S(2)}, u32[]{:S(2)}) collective-permute-start(bf16[32,2,1024]{2,1,0:T(2,128)(2,1)} %param.4), channel_id=1, source_target_pairs={{0,16},{16,32},{32,48},{48,64},{64,80},{80,96},{96,112},{112,128},... | collective-permute-start | bytes 393224 | tf_op jit(solution)/shard_map/ppermute | solution.py:16
  4.1 1.3 collective-permute-start.1
  5.4 0.8 copy.41
  6.2 0.7 compare_and_fusion.1
  6.9 1.1 copy.42
  8.0 0.0 copy-start.1
  8.0 0.1 reshape.225
  8.1 1.0 gather_fusion
  9.2 0.2 gather.16
  9.3 0.1 copy.53
  9.5 0.2 broadcast_in_dim.44.clone
  9.7 0.1 broadcast_in_dim.48
  9.8 0.1 compare_select_fusion
  10.0 0.1 gather.15
  10.1 0.1 copy.43
  10.2 0.1 copy.44
  10.4 0.0 collective-permute-done
  10.4 0.0 collective-permute-done.1
  10.4 0.0 copy-done.1
  10.4 0.3 pad_maximum_fusion.1
  10.8 0.1 reshape.226
  10.9 0.4 copy.46
  11.3 57.9 %gather_fusion.1 = bf16[16384,64]{1,0:T(8,128)(2,1)} fusion(bf16[64,3072]{0,1:T(8,128)(2,1)S(1)} %copy.46, s32[16384]{0:T(1024)S(1)} %broadcast_clamp_fusion), kind=kCustom, calls=%fused_computation.1 | custom fusion | bytes 4259840 | tf_op jit(solution)/shard_map/jit(_take)/gather | solution.py:41
  69.2 4.8 %copy.47 = bf16[64,16384]{1,0:T(8,128)(2,1)} copy(bf16[64,16384]{0,1:T(8,128)(2,1)} %bitcast.29) | data formatting | bytes 4194304 | tf_op jit(solution)/shard_map/jit(_take)/gather | solution.py:41
  74.0 2.2 %copy.54 = bf16[8,8,128,128]{3,2,1,0:T(8,128)(2,1)S(1)} copy(bf16[8,8,128,128]{3,1,2,0:T(8,128)(2,1)} %bitcast.30) | data formatting | bytes 4194304
  76.2 0.0 copy-done
  76.2 3.3 %convert_bitcast_fusion = bf16[32,2,256,128]{2,3,1,0:T(8,128)(2,1)} fusion(bf16[32,256,128]{2,1,0:T(8,128)(2,1)S(1)} %copy-done, bf16[32,2,128,128]{3,2,1,0:T(8,128)(2,1)S(1)} %bitcast.31, pred[128,128]{1,0:T(8,128)(4,1)S(1)} %copy.44), kind=kOutput, calls=%fused_computation.3 | convolution fusion | flops 540016640 | bytes 8404992 | tf_op jit(solution)/shard_map/dot_general | solution.py:44
  79.5 11.2 %copy.48 = bf16[32,2,256,128]{3,1,0,2:T(2,128)(2,1)} copy(bf16[32,2,256,128]{2,3,1,0:T(8,128)(2,1)} %convert_bitcast_fusion) | data formatting | bytes 8388608 | tf_op jit(solution)/shard_map/convert_element_type | solution.py:47
  90.7 9.2 %all-to-all-start = ((bf16[32,2,256,128]{3,1,0,2:T(2,128)(2,1)}), bf16[32,2,256,128]{3,1,0,2:T(2,128)(2,1)}, u32[]{:S(2)}, u32[]{:S(2)}) async-start(bf16[32,2,256,128]{3,1,0,2:T(2,128)(2,1)} %copy.48), calls=%async_computation | async-start | bytes 8388608 | tf_op jit(solution)/shard_map/all_to_all | solution.py:50
  99.9 8.7 %multiply_convert_fusion = (bf16[512,1,1024]{2,0,1:T(8,128)(2,1)S(1)}, bf16[512,1,1024]{2,0,1:T(8,128)(2,1)S(1)}) fusion(f32[512]{0:T(512)S(1)} %fusion.10, f32[512]{0:T(512)S(1)} %select_multiply_fusion), kind=kLoop, calls=%fused_computation.12 | loop fusion | flops 9437184 | bytes 2101248 | tf_op jit(solution)/shard_map/convert.1
  108.6 0.2 pad_maximum_fusion
  108.8 3.5 %copy.52 = bf16[512,2,1024]{2,1,0:T(2,128)(2,1)} copy(bf16[512,2,1024]{2,0,1:T(8,128)(2,1)S(1)} %pad_maximum_fusion) | data formatting | bytes 4194304 | tf_op jit(solution)/shard_map/stack | solution.py:30
  112.3 4.1 %reshape.244 = bf16[1024,1024,1]{1,0,2:T(8,128)(2,1)} reshape(bf16[512,2,1024]{2,1,0:T(2,128)(2,1)} %copy.52) | data formatting | bytes 4194304 | tf_op jit(solution)/shard_map/convert_element_type | solution.py:31
  116.4 34.7 %all-to-all-done = bf16[32,2,256,128]{3,1,0,2:T(2,128)(2,1)} async-done(((bf16[32,2,256,128]{3,1,0,2:T(2,128)(2,1)}), bf16[32,2,256,128]{3,1,0,2:T(2,128)(2,1)}, u32[]{:S(2)}, u32[]{:S(2)}) %all-to-all-start) | async-done | bytes 4194336 | tf_op jit(solution)/shard_map/all_to_all | solution.py:50
  151.1 7.0 %copy.49 = bf16[32,2,256,128]{3,2,1,0:T(8,128)(2,1)S(1)} copy(bf16[32,2,256,128]{3,1,0,2:T(2,128)(2,1)} %all-to-all-done) | data formatting | bytes 8388608 | tf_op jit(solution)/shard_map/all_to_all | solution.py:50
  158.1 1.1 copy.50
  159.2 4.1 %copy.57 = bf16[128,8,16,128]{3,1,2,0:T(8,128)(2,1)} copy(bf16[128,8,16,128]{3,2,1,0:T(8,128)(2,1)S(1)} %bitcast.27) | data formatting | bytes 8388608
  163.4 6.4 %copy.51 = bf16[2048,1024]{1,0:T(8,128)(2,1)} copy(bf16[2048,1024]{0,1:T(8,128)(2,1)} %bitcast.28) | data formatting | bytes 8388608 | tf_op jit(solution)/shard_map/dot_general | solution.py:54
  169.8 9.4 %convolution_convert_fusion = bf16[16,128,1024]{2,1,0:T(8,128)(2,1)} fusion(bf16[16,128,1024]{2,1,0:T(8,128)(2,1)} %bitcast.32, bf16[1024,1024,1]{1,0,2:T(8,128)(2,1)} %reshape.244), kind=kOutput, calls=%fused_computation.7 | convolution fusion | flops 4297064448 | bytes 10485760 | tf_op jit(solution)/shard_map/dot_general | solution.py:54
  (6 shorter events, 0.1 us)
Async XLA Ops:
  0.0 76.2 %copy-start = (bf16[32,256,128]{2,1,0:T(8,128)(2,1)S(1)}, bf16[32,256,128]{2,1,0:T(8,128)(2,1)}, u32[]{:S(2)}) copy-start(bf16[32,256,128]{2,1,0:T(8,128)(2,1)} %param.5) | copy-start | bytes 6291460
  0.0 10.4 %collective-permute-start = (bf16[32,2,1024]{2,1,0:T(2,128)(2,1)}, bf16[32,2,1024]{2,1,0:T(2,128)(2,1)S(1)}, u32[]{:S(2)}, u32[]{:S(2)}) collective-permute-start(bf16[32,2,1024]{2,1,0:T(2,128)(2,1)} %param.4), channel_id=1, source_target_pairs={{0,16},{16,32},{32,48},{48,64},{64,80},{80,96},{96,112},{112,128},... | collective-permute-start | bytes 393224 | tf_op jit(solution)/shard_map/ppermute | solution.py:16
  4.1 6.3 %collective-permute-start.1 = (bf16[32,2,1024]{2,1,0:T(2,128)(2,1)}, bf16[32,2,1024]{2,1,0:T(2,128)(2,1)S(1)}, u32[]{:S(2)}, u32[]{:S(2)}) collective-permute-start(bf16[32,2,1024]{2,1,0:T(2,128)(2,1)} %param.4), channel_id=1, source_target_pairs={{16,0},{32,16},{48,32},{64,48},{80,64},{96,80},{112,96},{128,112},... | collective-permute-start | bytes 393224 | tf_op jit(solution)/shard_map/ppermute | solution.py:17
  8.0 2.4 %copy-start.1 = (bf16[32,2,1024]{2,1,0:T(2,128)(2,1)S(1)}, bf16[32,2,1024]{2,1,0:T(2,128)(2,1)}, u32[]{:S(2)}) copy-start(bf16[32,2,1024]{2,1,0:T(2,128)(2,1)} %param.4) | copy-start | bytes 393220
  90.7 60.4 %all-to-all-start = ((bf16[32,2,256,128]{3,1,0,2:T(2,128)(2,1)}), bf16[32,2,256,128]{3,1,0,2:T(2,128)(2,1)}, u32[]{:S(2)}, u32[]{:S(2)}) async-start(bf16[32,2,256,128]{3,1,0,2:T(2,128)(2,1)} %copy.48), calls=%async_computation | async-start | bytes 8388608 | tf_op jit(solution)/shard_map/all_to_all | solution.py:50
where the time goes:
time: 182 us; the launch traced here: 179 us
  local copies, waits for them, and re-layouts  107 us (59%)
  waiting for transfers between devices  34.7 us (19%)
  starting transfers between devices  14.6 us (8%)
  matrix products  12.7 us (7%)
  other arithmetic  10.1 us (6%)
    gather x2, local copies, waits for them, and re-layouts, shards(): picked = jnp.take(flat_source, local_ids.reshape(-1), axis=1)  62.7 us
    all_to_all x1, waiting for transfers between devices, shards(): lax.all_to_all(field, 'mode', split_axis=2, concat_axis=0, tiled=True)  34.7 us
    convert_element_type x1, local copies, waits for them, and re-layouts, shards(): field = field.astype(jnp.bfloat16)  11.2 us
    dot_general x1, matrix products, shards(): lax.dot_general(flat, table, (((0,), (0,)), ((), ())), preferred_element_...  9.41 us
    all_to_all x1, starting transfers between devices, shards(): lax.all_to_all(field, 'mode', split_axis=2, concat_axis=0, tiled=True)  9.25 us
    another operation x1, other arithmetic  8.68 us
    unnamed x9, local copies, waits for them, and re-layouts  8.32 us
    all_to_all x2, local copies, waits for them, and re-layouts, shards(): lax.all_to_all(field, 'mode', split_axis=2, concat_axis=0, tiled=True)  8.13 us
  transfers between devices with their start and end apart: 3, of which 1 were waited for; matrix products, arithmetic and copies ran while one was open for 12% of the time, Pallas kernels for 0%

commit v1 on v0

v1 whole, which is shorter than its diff:
```python
import math

import jax
import jax.numpy as jnp
from jax import lax
from jax.experimental import pallas as pl
from jax.experimental.pallas import tpu as pltpu
from jax.sharding import PartitionSpec as P

BF16 = jnp.bfloat16
F32 = jnp.float32
LANES = 128
SUBS = 8


def half_table(modes):
    angles = 2 * modes
    row = lax.broadcasted_iota(jnp.int32, (2 * modes, modes), 0)
    angle = lax.broadcasted_iota(jnp.int32, (2 * modes, modes), 1)
    parity = row // modes
    rest = row % modes
    order = (rest // 2) * 2 + parity
    phase = (order * angle % angles).astype(F32) * (2.0 * math.pi / angles)
    weight = jnp.where(order == 0, 1.0, 2.0).astype(F32) / math.sqrt(2.0 * modes)
    return jnp.where(rest % 2 == 0, weight * jnp.cos(phase), -weight * jnp.sin(phase)).astype(BF16)


def order_kernel(width, tile_ref, charges_ref, skel_ref, out_ref, hot, rows):
    slots, boxes = skel_ref.shape[0], slots_boxes(width, skel_ref.shape[0])
    tile = tile_ref[0]
    per_block = LANES // boxes
    groups = slots // SUBS
    lane = lax.broadcasted_iota(jnp.int32, (SUBS, LANES), 1)
    index = jnp.zeros((SUBS, LANES), jnp.int32)
    for u in range(groups):
        part = skel_ref[u * SUBS : (u + 1) * SUBS, :]
        shift = lax.rem(u * boxes - lax.rem(tile, per_block) * boxes + LANES, LANES)
        moved = pltpu.roll(part, shift, 1)
        index = jnp.where(lane // boxes == u, moved, index)
    index = index - tile * width
    spot = lax.broadcasted_iota(jnp.int32, (width, LANES), 0)
    for q in range(SUBS):
        hot[:, q * LANES : (q + 1) * LANES] = jnp.where(spot == index[q : q + 1, :], 1.0, 0.0).astype(BF16)
    count = charges_ref.shape[0]
    moved = jnp.dot(charges_ref[...], hot[...], preferred_element_type=F32)
    for q in range(SUBS):
        rows[pl.ds(q, count, stride=SUBS), :] = moved[:, q * LANES : (q + 1) * LANES]
    out_ref[...] = rows[...].astype(BF16)


def slots_boxes(width, slots):
    return width // slots


def box_order(charges, skel_t, tile):
    count, width = charges.shape
    slots = skel_t.shape[0]
    per_block = LANES // slots_boxes(width, slots)
    rows = count * SUBS

    def body(tile_ref, charges_ref, skel_ref, out_ref, hot, scratch):
        order_kernel(width, tile_ref, charges_ref, skel_ref, out_ref, hot, scratch)

    return pl.pallas_call(
        body,
        out_shape=jax.ShapeDtypeStruct((rows, LANES), BF16),
        grid_spec=pltpu.PrefetchScalarGridSpec(
            num_scalar_prefetch=1,
            grid=(1,),
            in_specs=[
                pl.BlockSpec((count, width), lambda i, t: (0, 0)),
                pl.BlockSpec((slots, LANES), lambda i, t: (0, t[0] // per_block)),
            ],
            out_specs=pl.BlockSpec((rows, LANES), lambda i, t: (0, 0)),
            scratch_shapes=[pltpu.VMEM((width, width), BF16), pltpu.VMEM((rows, LANES), F32)],
        ),
        compiler_params=pltpu.CompilerParams(vmem_limit_bytes=32 * 2**20),
    )(tile.reshape(1), charges, skel_t)


def field_kernel(boxes, tile_ref, before, own, after, lists_ref, proxy_ref, out_ref, hot, picked, total):
    modes, targets, depth = proxy_ref.shape
    lists, tiles = lists_ref.shape
    groups = LANES // boxes
    cols = lists * tiles
    base = (tile_ref[0] - 1) * boxes
    hot[...] = jnp.zeros_like(hot)
    box = lax.broadcasted_iota(jnp.int32, (boxes, tiles), 0)
    for o in range(3):
        for l in range(lists):
            want = lists_ref[l : l + 1, :] - (base + o * boxes)
            block = jnp.where(box == want, 1.0, 0.0).astype(BF16)
            for u in range(groups):
                hot[
                    o * LANES + u * boxes : o * LANES + (u + 1) * boxes,
                    u * cols + l * tiles : u * cols + (l + 1) * tiles,
                ] = block
    source = jnp.concatenate([before[...], own[...], after[...]], axis=1)
    for h in range(groups // 2):
        got = jnp.dot(source, hot[:, 2 * h * cols : 2 * (h + 1) * cols], preferred_element_type=F32)
        got = got.reshape(modes, 2, SUBS, 2 * cols)
        for l in range(lists):
            low = got[..., l * tiles : (l + 1) * tiles]
            high = got[..., cols + l * tiles : cols + (l + 1) * tiles]
            both = jnp.concatenate([low, high], axis=2).astype(BF16)
            first = l * (groups * SUBS) + h * 2 * SUBS
            for c in range(2):
                picked[:, first : first + 2 * SUBS, c * tiles : (c + 1) * tiles] = both[:, c]
    stride = 2 * modes

    def one(m, carry):
        res = jnp.dot(proxy_ref[m], picked[m], preferred_element_type=F32)
        row = lax.rem(m, 2) * modes + (m // 2) * 2
        for c in range(2):
            total[pl.ds(row + c, targets, stride=stride), :] = res[:, c * tiles : (c + 1) * tiles]
        return carry

    lax.fori_loop(0, modes, one, 0, unroll=4)
    out_ref[...] = total[...].astype(BF16)


def fields(before, own, after, lists, proxy, tile, boxes):
    modes, targets, depth = proxy.shape
    rows = targets * 2 * modes
    groups = LANES // boxes
    tiles = lists.shape[1]

    def body(*refs):
        field_kernel(boxes, *refs)

    whole = pl.BlockSpec(memory_space=pltpu.VMEM)
    return pl.pallas_call(
        body,
        out_shape=jax.ShapeDtypeStruct((rows, tiles), BF16),
        in_specs=[pl.BlockSpec(memory_space=pltpu.SMEM)] + [whole] * 5,
        out_specs=whole,
        scratch_shapes=[
            pltpu.VMEM((3 * LANES, groups * lists.shape[0] * tiles), BF16),
            pltpu.VMEM((modes, depth, 2 * tiles), BF16),
            pltpu.VMEM((rows, tiles), F32),
        ],
        compiler_params=pltpu.CompilerParams(vmem_limit_bytes=40 * 2**20),
    )(tile.reshape(1), before, own, after, lists, proxy)


def synth_kernel(block_ref, table_ref, out_ref):
    peers, targets, rows, tiles = block_ref.shape
    half = rows // 2
    for p in range(targets):
        sums = []
        for parity in range(2):
            part = block_ref[:, p, parity * half : (parity + 1) * half, :].reshape(peers * half, tiles)
            weights = table_ref[parity * peers * half : (parity + 1) * peers * half, :]
            sums.append(
                lax.dot_general(part, weights, (((0,), (0,)), ((), ())), preferred_element_type=F32)
            )
        width = sums[0].shape[1]
        out_ref[p, :, :width] = (sums[0] + sums[1]).astype(BF16)
        out_ref[p, :, width:] = (sums[0] - sums[1]).astype(BF16)


def synthesis(block, table, step):
    peers, targets, rows, tiles = block.shape
    angles = 2 * table.shape[1]
    return pl.pallas_call(
        synth_kernel,
        out_shape=jax.ShapeDtypeStruct((targets, tiles, angles), BF16),
        grid=(targets // step,),
        in_specs=[
            pl.BlockSpec((peers, step, rows, tiles), lambda i: (0, i, 0, 0)),
            pl.BlockSpec(table.shape, lambda i: (0, 0)),
        ],
        out_specs=pl.BlockSpec((step, tiles, angles), lambda i: (i, 0, 0)),
        compiler_params=pltpu.CompilerParams(vmem_limit_bytes=32 * 2**20),
    )(block, table)


def shards(charges, proxy, tile_boxes, box_skel):
    modes_here, parts, skel_here = charges.shape
    _, targets, _ = proxy.shape
    tiles_here, _ = tile_boxes.shape
    slots = box_skel.shape[1]
    peers = lax.axis_size("mode")
    groups = lax.axis_size("tile")
    tile = lax.axis_index("tile").astype(jnp.int32)
    own = box_order(charges.reshape(modes_here * parts, skel_here), box_skel.T, tile)
    up = [(i, (i + 1) % groups) for i in range(groups)]
    before = lax.ppermute(own, "tile", up)
    after = lax.ppermute(own, "tile", [(j, i) for i, j in up])
    field = fields(before, own, after, tile_boxes.T, proxy, tile, skel_here // slots)
    width = targets // peers
    field = field.reshape(peers, width, modes_here * parts, tiles_here)
    block = lax.all_to_all(field, "mode", split_axis=0, concat_axis=0, tiled=True)
    table = half_table(modes_here * peers)
    return synthesis(block, table, 4)


def solution(mesh):
    placed = (P("mode", None, "tile"), P("mode", None, None), P("tile", None), P())
    return jax.shard_map(
        shards, mesh=mesh, in_specs=placed, out_specs=P("mode", "tile", None), check_vma=False
    )
```

time: 182 us -> 100 us (0.55); the launches traced: 179 us -> 99.9 us
  local copies, waits for them, and re-layouts: 107 us -> 6.13 us
  Pallas kernels: 0 us -> 17.4 us
  matrix products: 12.7 us -> 0 us
  starting transfers between devices: 14.6 us -> 23 us
  waiting for transfers between devices: 34.7 us -> 42.5 us
    gather x6 -> x0, local copies, waits for them, and re-layouts: 64.1 us -> none  [the longest x2 62.7 us: shards(): picked = jnp.take(flat_source, local_ids.reshape(-1), axis=1)]
    pallas_call x0 -> x3, Pallas kernels: none -> 17.4 us  [the longest x1 10.2 us: fields(): pl.pallas_call(body, out_shape=jax.ShapeDtypeStruct((rows, tiles), BF16),...]
    convert_element_type x2 -> x0, local copies, waits for them, and re-layouts: 15.4 us -> none  [the longest x1 11.2 us: shards(): field = field.astype(jnp.bfloat16)]
    dot_general x2 -> x0, matrix products: 12.7 us -> none  [the longest x1 9.41 us: shards(): lax.dot_general(flat, table, (((0,), (0,)), ((), ())), preferred_element_...]
    convert_element_type x0 -> x1, other arithmetic: none -> 10.7 us  [half_table(): jnp.where(rest % 2 == 0, weight * jnp.cos(phase), -weight * jnp.sin(phase))]
    ppermute x2, starting transfers between devices: 5.37 us -> 14.8 us  [the longest x1 10.9 us: shards(): after = lax.ppermute(own, 'tile', [(j, i) for i, j in up])]
    another operation x2 -> x0, other arithmetic: 8.88 us -> none
    all_to_all x2 -> x0, local copies, waits for them, and re-layouts: 8.13 us -> none  [shards(): lax.all_to_all(field, 'mode', split_axis=2, concat_axis=0, tiled=True)]
  transfers between devices with their start and end apart: 3 -> 3, of which waited for: 1 -> 3; matrix products, arithmetic and copies ran while one was open for 12% -> 11% of each run, Pallas kernels for 0% -> 0%
where the time goes in v1:
time: 100 us; the launch traced here: 99.9 us
  waiting for transfers between devices  42.5 us (42%)
  starting transfers between devices  23 us (23%)
  Pallas kernels  17.4 us (17%)
  other arithmetic  10.7 us (11%)
  local copies, waits for them, and re-layouts  6.13 us (6%)
    all_to_all x1, waiting for transfers between devices, shards(): lax.all_to_all(field, 'mode', split_axis=0, concat_axis=0, tiled=True)  40.3 us
    ppermute x1, starting transfers between devices, shards(): after = lax.ppermute(own, 'tile', [(j, i) for i, j in up])  10.9 us
    convert_element_type x1, other arithmetic, half_table(): jnp.where(rest % 2 == 0, weight * jnp.cos(phase), -weight * jnp.sin(phase))  10.7 us
    pallas_call x1, Pallas kernels, fields(): pl.pallas_call(body, out_shape=jax.ShapeDtypeStruct((rows, tiles), BF16),...  10.2 us
    all_to_all x1, starting transfers between devices, shards(): lax.all_to_all(field, 'mode', split_axis=0, concat_axis=0, tiled=True)  8.19 us
    pallas_call x1, Pallas kernels, synthesis(): pl.pallas_call(synth_kernel, out_shape=jax.ShapeDtypeStruct((targets, til...  6.16 us
    unnamed x8, local copies, waits for them, and re-layouts  5.18 us
    ppermute x1, starting transfers between devices, shards(): before = lax.ppermute(own, 'tile', up)  3.95 us
  transfers between devices with their start and end apart: 3, of which 3 were waited for; matrix products, arithmetic and copies ran while one was open for 11% of the time, Pallas kernels for 0%

profile of v1, /device:TPU:1, one launch (start us, length us, event | category | flops | bytes accessed | tf_op | source)
XLA Modules:
  0.0 99.9 jit_solution(7416337342147172902)
XLA Ops:
  0.0 1.0 reshape.11.charges_ref
  1.0 0.0 copy-start.2
  1.0 0.9 copy-done.2
  1.9 1.1 %shard_map.46.refs_2_ = bf16[512,128]{1,0:T(8,128)(2,1)S(1)} custom-call(s32[1]{0:T(128)} %bitcast.tile_ref.refs_0_, bf16[64,1024]{1,0:T(8,128)(2,1)S(1)} %reshape.11.charges_ref, s32[32,1024]{1,0:T(8,128)S(1)} %bitcast.5), custom_call_target="tpu_custom_call" | custom-call | tf_op jit(solution)/shard_map/pallas_call | solution.py:64
  2.9 3.9 %collective-permute-start = (bf16[512,128]{1,0:T(8,128)(2,1)S(1)}, bf16[512,128]{1,0:T(8,128)(2,1)S(1)}, u32[]{:S(2)}, u32[]{:S(2)}) collective-permute-start(bf16[512,128]{1,0:T(8,128)(2,1)S(1)} %shard_map.46.refs_2_), channel_id=1, source_target_pairs={{0,16},{16,32},{32,48},{48,64},{64,80},{80,96},{96,112},{112,128},... | collective-permute-start | bytes 393224 | tf_op jit(solution)/shard_map/ppermute | solution.py:188
  6.9 10.9 %collective-permute-start.1 = (bf16[512,128]{1,0:T(8,128)(2,1)S(1)}, bf16[512,128]{1,0:T(8,128)(2,1)S(1)}, u32[]{:S(2)}, u32[]{:S(2)}) collective-permute-start(bf16[512,128]{1,0:T(8,128)(2,1)S(1)} %shard_map.46.refs_2_), channel_id=1, source_target_pairs={{16,0},{32,16},{48,32},{64,48},{80,64},{96,80},{112,96},{128,112},... | collective-permute-start | bytes 393224 | tf_op jit(solution)/shard_map/ppermute | solution.py:189
  17.7 1.3 %collective-permute-done.refs_1_ = bf16[512,128]{1,0:T(8,128)(2,1)S(1)} collective-permute-done((bf16[512,128]{1,0:T(8,128)(2,1)S(1)}, bf16[512,128]{1,0:T(8,128)(2,1)S(1)}, u32[]{:S(2)}, u32[]{:S(2)}) %collective-permute-start) | collective-permute-done | bytes 131104 | tf_op jit(solution)/shard_map/ppermute | solution.py:188
  19.0 0.9 collective-permute-done.1.refs_3_
  19.9 0.0 copy-start.1
  19.9 1.6 %copy-done.1 = bf16[32,256,128]{2,1,0:T(8,128)(2,1)S(1)} copy-done((bf16[32,256,128]{2,1,0:T(8,128)(2,1)S(1)}, bf16[32,256,128]{2,1,0:T(8,128)(2,1)}, u32[]{:S(2)}) %copy-start.1) | copy-done | bytes 2097176
  21.5 0.0 copy-start.3
  21.5 0.7 copy-done.3
  22.2 10.2 %shard_map.47 = bf16[16384,128]{1,0:T(8,128)(2,1)S(1)} custom-call(s32[1]{0:T(128)} %bitcast.tile_ref.refs_0_, bf16[512,128]{1,0:T(8,128)(2,1)S(1)} %collective-permute-done.refs_1_, bf16[512,128]{1,0:T(8,128)(2,1)S(1)} %shard_map.46.refs_2_, bf16[512,128]{1,0:T(8,128)(2,1)S(1)} %collective-permute-done.1.refs_3_, s32[4,128]{1,0:T(4,128)S(1)} %bitcast.6, ...), custom_call_target="tpu_custom_call" | custom-call | tf_op jit(solution)/shard_map/pallas_call | solution.py:132
  32.4 0.0 copy-start
  32.4 2.0 %copy-done = bf16[16384,128]{1,0:T(8,128)(2,1)} copy-done((bf16[16384,128]{1,0:T(8,128)(2,1)}, bf16[16384,128]{1,0:T(8,128)(2,1)S(1)}, u32[]{:S(2)}) %copy-start) | copy-done | bytes 4194328
  34.4 8.2 %all-to-all-start = ((bf16[16,16,64,128]{3,2,1,0:T(8,128)(2,1)}), bf16[16,16,64,128]{3,2,1,0:T(8,128)(2,1)}, u32[]{:S(2)}, u32[]{:S(2)}) async-start(bf16[16,16,64,128]{3,2,1,0:T(8,128)(2,1)} %bitcast.4), calls=%async_computation | async-start | bytes 8388608 | tf_op jit(solution)/shard_map/all_to_all | solution.py:193
  42.6 10.7 %select_convert_fusion.table_ref = bf16[1024,512]{1,0:T(8,128)(2,1)S(1)} fusion(s32[1024]{0:T(1024)S(1)} %get-tuple-element.5, s32[1024]{0:T(1024)S(1)} %get-tuple-element.8, s32[1024]{0:T(1024)S(1)} %get-tuple-element.6, s32[1024]{0:T(1024)S(1)} %get-tuple-element.7, pred[1024]{0:T(1024)(128)(4,1)S(1)} %get-tuple-element.9, ...), kind=kLoop, calls=%fused_computation.20 | loop fusion | flops 24117248 | bytes 1067008 | tf_op jit(solution)/shard_map/convert_element_type | solution.py:25
  53.4 40.3 %all-to-all-done.block_ref = bf16[16,16,64,128]{3,2,1,0:T(8,128)(2,1)} async-done(((bf16[16,16,64,128]{3,2,1,0:T(8,128)(2,1)}), bf16[16,16,64,128]{3,2,1,0:T(8,128)(2,1)}, u32[]{:S(2)}, u32[]{:S(2)}) %all-to-all-start) | async-done | bytes 4194336 | tf_op jit(solution)/shard_map/all_to_all | solution.py:193
  93.7 6.2 %shard_map.48 = bf16[16,128,1024]{2,1,0:T(8,128)(2,1)} custom-call(bf16[16,16,64,128]{3,2,1,0:T(8,128)(2,1)} %all-to-all-done.block_ref, bf16[1024,512]{1,0:T(8,128)(2,1)S(1)} %select_convert_fusion.table_ref), custom_call_target="tpu_custom_call" | custom-call | tf_op jit(solution)/shard_map/pallas_call | solution.py:165
  (3 shorter events, 0.0 us)
Async XLA Ops:
  1.0 0.9 copy-start.2
  2.9 16.1 %collective-permute-start = (bf16[512,128]{1,0:T(8,128)(2,1)S(1)}, bf16[512,128]{1,0:T(8,128)(2,1)S(1)}, u32[]{:S(2)}, u32[]{:S(2)}) collective-permute-start(bf16[512,128]{1,0:T(8,128)(2,1)S(1)} %shard_map.46.refs_2_), channel_id=1, source_target_pairs={{0,16},{16,32},{32,48},{48,64},{64,80},{80,96},{96,112},{112,128},... | collective-permute-start | bytes 393224 | tf_op jit(solution)/shard_map/ppermute | solution.py:188
  6.9 13.0 %collective-permute-start.1 = (bf16[512,128]{1,0:T(8,128)(2,1)S(1)}, bf16[512,128]{1,0:T(8,128)(2,1)S(1)}, u32[]{:S(2)}, u32[]{:S(2)}) collective-permute-start(bf16[512,128]{1,0:T(8,128)(2,1)S(1)} %shard_map.46.refs_2_), channel_id=1, source_target_pairs={{16,0},{32,16},{48,32},{64,48},{80,64},{96,80},{112,96},{128,112},... | collective-permute-start | bytes 393224 | tf_op jit(solution)/shard_map/ppermute | solution.py:189
  19.9 1.6 %copy-start.1 = (bf16[32,256,128]{2,1,0:T(8,128)(2,1)S(1)}, bf16[32,256,128]{2,1,0:T(8,128)(2,1)}, u32[]{:S(2)}) copy-start(bf16[32,256,128]{2,1,0:T(8,128)(2,1)} %refs_5_.1) | copy-start | bytes 6291460
  21.5 0.7 copy-start.3
  32.4 2.0 %copy-start = (bf16[16384,128]{1,0:T(8,128)(2,1)}, bf16[16384,128]{1,0:T(8,128)(2,1)S(1)}, u32[]{:S(2)}) copy-start(bf16[16384,128]{1,0:T(8,128)(2,1)S(1)} %shard_map.47) | copy-start | bytes 12582916
  34.4 59.3 %all-to-all-start = ((bf16[16,16,64,128]{3,2,1,0:T(8,128)(2,1)}), bf16[16,16,64,128]{3,2,1,0:T(8,128)(2,1)}, u32[]{:S(2)}, u32[]{:S(2)}) async-start(bf16[16,16,64,128]{3,2,1,0:T(8,128)(2,1)} %bitcast.4), calls=%async_computation | async-start | bytes 8388608 | tf_op jit(solution)/shard_map/all_to_all | solution.py:193

commit v2 on v1

v2 whole, which is shorter than its diff:
```python
import math

import jax
import jax.numpy as jnp
from jax import lax
from jax.experimental import pallas as pl
from jax.experimental.pallas import tpu as pltpu
from jax.sharding import PartitionSpec as P

BF16 = jnp.bfloat16
F32 = jnp.float32
LANES = 128
SUBS = 8
ROWS16 = 16
MIB = 2**20


def half_table(modes):
    angles = 2 * modes
    row = lax.broadcasted_iota(jnp.int32, (2 * modes, modes), 0)
    angle = lax.broadcasted_iota(jnp.int32, (2 * modes, modes), 1)
    parity = row // modes
    rest = row % modes
    order = (rest // 2) * 2 + parity
    phase = (order * angle % angles).astype(F32) * (2.0 * math.pi / angles)
    weight = jnp.where(order == 0, 1.0, 2.0).astype(F32) / math.sqrt(2.0 * modes)
    return jnp.where(rest % 2 == 0, weight * jnp.cos(phase), -weight * jnp.sin(phase)).astype(BF16)


def order_kernel(boxes, charges_hbm, skel_hbm, out_ref, charges, skel, hot, rows, sems):
    modes, parts, width = charges.shape
    slots = skel.shape[0]
    tile = lax.axis_index("tile")
    per_block = LANES // boxes
    column = pl.multiple_of(tile // per_block * LANES, LANES)
    skel_copy = pltpu.make_async_copy(skel_hbm.at[:, pl.ds(column, LANES)], skel, sems.at[0])
    charges_copy = pltpu.make_async_copy(charges_hbm, charges, sems.at[1])
    skel_copy.start()
    charges_copy.start()
    spot = lax.broadcasted_iota(jnp.int32, (width, LANES), 0)
    lane = lax.broadcasted_iota(jnp.int32, (SUBS, LANES), 1)
    skel_copy.wait()
    index = jnp.zeros((SUBS, LANES), jnp.int32)
    for u in range(slots // SUBS):
        shift = lax.rem(u * boxes - lax.rem(tile, per_block) * boxes + LANES, LANES)
        moved = pltpu.roll(skel[u * SUBS : (u + 1) * SUBS, :], shift, 1)
        index = jnp.where(lane // boxes == u, moved, index)
    index = index - tile * width
    for q in range(SUBS):
        hot[:, q * LANES : (q + 1) * LANES] = jnp.where(spot == index[q : q + 1, :], 1.0, 0.0).astype(BF16)
    charges_copy.wait()
    count = modes * parts
    held = charges[...].reshape(count, width)
    moved = jnp.dot(held, hot[...], preferred_element_type=F32)
    for q in range(SUBS):
        rows[pl.ds(q, count, stride=SUBS), :] = moved[:, q * LANES : (q + 1) * LANES]
    out_ref[...] = rows[...].astype(BF16)


def box_order(charges, skel_t):
    modes, parts, width = charges.shape
    slots = skel_t.shape[0]
    boxes = width // slots
    rows = modes * parts * SUBS

    def body(*refs):
        order_kernel(boxes, *refs)

    return pl.pallas_call(
        body,
        out_shape=jax.ShapeDtypeStruct((rows, LANES), BF16),
        in_specs=[pl.BlockSpec(memory_space=pl.ANY)] * 2,
        out_specs=pl.BlockSpec(memory_space=pltpu.VMEM),
        scratch_shapes=[
            pltpu.VMEM((modes, parts, width), BF16),
            pltpu.VMEM((slots, LANES), jnp.int32),
            pltpu.VMEM((width, width), BF16),
            pltpu.VMEM((rows, LANES), F32),
            pltpu.SemaphoreType.DMA((2,)),
        ],
        compiler_params=pltpu.CompilerParams(vmem_limit_bytes=32 * MIB),
    )(charges, skel_t)


def field_kernel(boxes, near, own, far, lists_hbm, proxy_hbm, out_hbm, lists, proxy, hot, picked, field, sems):
    modes, targets, depth = proxy.shape
    count, tiles = lists.shape
    groups = LANES // boxes
    cols = count * tiles
    lists_copy = pltpu.make_async_copy(lists_hbm, lists, sems.at[0])
    proxy_copy = pltpu.make_async_copy(proxy_hbm, proxy, sems.at[1])
    lists_copy.start()
    proxy_copy.start()
    hot[...] = jnp.zeros_like(hot)
    tile = lax.axis_index("tile")
    toward = 1 - 2 * lax.rem(tile, 2)
    box = lax.broadcasted_iota(jnp.int32, (boxes, tiles), 0)
    lists_copy.wait()
    for o, owner in enumerate((tile + toward, tile, tile - toward)):
        for l in range(count):
            want = lists[l : l + 1, :] - owner * boxes
            block = jnp.where(box == want, 1.0, 0.0).astype(BF16)
            for u in range(groups):
                hot[
                    o * LANES + u * boxes : o * LANES + (u + 1) * boxes,
                    u * cols + l * tiles : u * cols + (l + 1) * tiles,
                ] = block
    source = jnp.concatenate([near[...], own[...], far[...]], axis=1)
    for h in range(groups // 2):
        got = jnp.dot(source, hot[:, 2 * h * cols : 2 * (h + 1) * cols], preferred_element_type=F32)
        got = got.reshape(modes, 2, SUBS, 2 * cols)
        for l in range(count):
            low = got[..., l * tiles : (l + 1) * tiles]
            high = got[..., cols + l * tiles : cols + (l + 1) * tiles]
            both = jnp.concatenate([low, high], axis=2).astype(BF16)
            first = l * (groups * SUBS) + h * 2 * SUBS
            for c in range(2):
                picked[:, first : first + 2 * SUBS, c * tiles : (c + 1) * tiles] = both[:, c]
    proxy_copy.wait()
    per = ROWS16 // 2
    half = modes // 2
    writes = []
    for g in range(modes // per):
        parts = []
        for j in range(per):
            m = g // (half // per) + 2 * (g % (half // per) * per + j)
            res = jnp.dot(proxy[m], picked[m], preferred_element_type=F32).astype(BF16)
            parts += [res[:, :tiles], res[:, tiles:]]
        span = slice(g * ROWS16, (g + 1) * ROWS16)
        field[:, span, :] = jnp.swapaxes(jnp.stack(parts, axis=0), 0, 1)
        copy = pltpu.make_async_copy(field.at[:, span, :], out_hbm.at[:, span, :], sems.at[2 + g])
        copy.start()
        writes.append(copy)
    for copy in writes:
        copy.wait()


def fields(near, own, far, lists, proxy, boxes):
    modes, targets, depth = proxy.shape
    count, tiles = lists.shape
    groups = LANES // boxes

    def body(*refs):
        field_kernel(boxes, *refs)

    held = pl.BlockSpec(memory_space=pltpu.VMEM)
    placed = pl.BlockSpec(memory_space=pl.ANY)
    shape = (targets, 2 * modes, tiles)
    return pl.pallas_call(
        body,
        out_shape=jax.ShapeDtypeStruct(shape, BF16),
        in_specs=[held] * 3 + [placed] * 2,
        out_specs=placed,
        scratch_shapes=[
            pltpu.VMEM((count, tiles), jnp.int32),
            pltpu.VMEM(proxy.shape, BF16),
            pltpu.VMEM((3 * LANES, groups * count * tiles), BF16),
            pltpu.VMEM((modes, depth, 2 * tiles), BF16),
            pltpu.VMEM(shape, BF16),
            pltpu.SemaphoreType.DMA((2 + 2 * modes // ROWS16,)),
        ],
        compiler_params=pltpu.CompilerParams(vmem_limit_bytes=40 * MIB),
    )(near, own, far, lists, proxy)


def synth_kernel(block_ref, table_ref, out_ref):
    peers, step, rows, tiles = block_ref.shape
    half = rows // 2
    depth = peers * half
    sums = []
    for parity in range(2):
        parts = [
            block_ref[:, p, parity * half : (parity + 1) * half, :].reshape(depth, tiles) for p in range(step)
        ]
        weights = table_ref[parity * depth : (parity + 1) * depth, :]
        sums.append(
            lax.dot_general(
                jnp.concatenate(parts, axis=1), weights, (((0,), (0,)), ((), ())), preferred_element_type=F32
            )
        )
    even, odd = sums
    width = even.shape[1]
    out_ref[:, :, :width] = (even + odd).astype(BF16).reshape(step, tiles, width)
    out_ref[:, :, width:] = (even - odd).astype(BF16).reshape(step, tiles, width)


def synthesis(block, table, step):
    peers, targets, rows, tiles = block.shape
    angles = 2 * table.shape[1]
    return pl.pallas_call(
        synth_kernel,
        out_shape=jax.ShapeDtypeStruct((targets, tiles, angles), BF16),
        grid=(targets // step,),
        in_specs=[
            pl.BlockSpec((peers, step, rows, tiles), lambda i: (0, i, 0, 0)),
            pl.BlockSpec(table.shape, lambda i: (0, 0)),
        ],
        out_specs=pl.BlockSpec((step, tiles, angles), lambda i: (i, 0, 0)),
        compiler_params=pltpu.CompilerParams(vmem_limit_bytes=40 * MIB),
    )(block, table)


def shards(charges, proxy, tile_boxes, box_skel):
    modes_here, parts, skel_here = charges.shape
    _, targets, _ = proxy.shape
    tiles_here, _ = tile_boxes.shape
    slots = box_skel.shape[1]
    peers = lax.axis_size("mode")
    groups = lax.axis_size("tile")
    own = box_order(charges, box_skel.T)
    far = lax.ppermute(own, "tile", [(i, (i - 1 + 2 * (i % 2)) % groups) for i in range(groups)])
    near = lax.ppermute(own, "tile", [(i, i + 1 - 2 * (i % 2)) for i in range(groups)])
    field = fields(near, own, far, tile_boxes.T, proxy, skel_here // slots)
    field = field.reshape(peers, targets // peers, modes_here * parts, tiles_here)
    block = lax.all_to_all(field, "mode", split_axis=0, concat_axis=0, tiled=True)
    table = half_table(modes_here * peers)
    return synthesis(block, table, 4)


def solution(mesh):
    placed = (P("mode", None, "tile"), P("mode", None, None), P("tile", None), P())
    return jax.shard_map(
        shards, mesh=mesh, in_specs=placed, out_specs=P("mode", "tile", None), check_vma=False
    )
```

time: 100 us -> 96.9 us (0.969)
  Pallas kernels: 17.4 us -> 12.9 us
    pallas_call x1, Pallas kernels: 10.2 us -> 4.78 us  [fields(): pl.pallas_call(body, out_shape=jax.ShapeDtypeStruct(shape, BF16), in_spec...]
    unnamed x8 -> x10, local copies, waits for them, and re-layouts: 5.18 us -> 6.09 us
  transfers between devices with their start and end apart: 3 -> 3, of which waited for: 3 -> 2; matrix products, arithmetic and copies ran while one was open for 11% -> 11% of each run, Pallas kernels for 0% -> 0%
where the time goes in v2:
time: 96.9 us; the launch traced here: 96.5 us
  waiting for transfers between devices  43.2 us (45%)
  starting transfers between devices  23.5 us (24%)
  Pallas kernels  12.9 us (13%)
  other arithmetic  10.7 us (11%)
  local copies, waits for them, and re-layouts  6.09 us (6%)
    all_to_all x1, waiting for transfers between devices, shards(): lax.all_to_all(field, 'mode', split_axis=0, concat_axis=0, tiled=True)  40.3 us
    ppermute x1, starting transfers between devices, shards(): lax.ppermute(own, 'tile', [(i, (i - 1 + 2 * (i % 2)) % groups) for i in r...  11.1 us
    convert_element_type x1, other arithmetic, half_table(): jnp.where(rest % 2 == 0, weight * jnp.cos(phase), -weight * jnp.sin(phase))  10.7 us
    all_to_all x1, starting transfers between devices, shards(): lax.all_to_all(field, 'mode', split_axis=0, concat_axis=0, tiled=True)  8.49 us
    pallas_call x1, Pallas kernels, synthesis(): pl.pallas_call(synth_kernel, out_shape=jax.ShapeDtypeStruct((targets, til...  6.13 us
    unnamed x10, local copies, waits for them, and re-layouts  6.09 us
    pallas_call x1, Pallas kernels, fields(): pl.pallas_call(body, out_shape=jax.ShapeDtypeStruct(shape, BF16), in_spec...  4.78 us
    ppermute x1, starting transfers between devices, shards(): lax.ppermute(own, 'tile', [(i, i + 1 - 2 * (i % 2)) for i in range(groups)])  3.95 us
  transfers between devices with their start and end apart: 3, of which 2 were waited for; matrix products, arithmetic and copies ran while one was open for 11% of the time, Pallas kernels for 0%

profile of v2, /device:TPU:1, one launch (start us, length us, event | category | flops | bytes accessed | tf_op | source)
XLA Modules:
  0.0 96.5 jit_solution(2098883183226402661)
XLA Ops:
  0.0 0.0 copy-start.2
  0.0 0.9 copy-done.2
  0.9 0.0 copy-start.3
  0.9 0.9 copy-done.3
  1.8 2.0 %shard_map.46.refs_1_ = bf16[512,128]{1,0:T(8,128)(2,1)S(1)} custom-call(bf16[32,2,1024]{2,1,0:T(2,128)(2,1)S(1)} %copy-done.2, s32[32,1024]{1,0:T(8,128)S(1)} %bitcast.4), custom_call_target="tpu_custom_call" | custom-call | tf_op jit(solution)/shard_map/pallas_call | solution.py:69
  3.8 3.9 %collective-permute-start = (bf16[512,128]{1,0:T(8,128)(2,1)S(1)}, bf16[512,128]{1,0:T(8,128)(2,1)S(1)}, u32[]{:S(2)}, u32[]{:S(2)}) collective-permute-start(bf16[512,128]{1,0:T(8,128)(2,1)S(1)} %shard_map.46.refs_1_), channel_id=1, source_target_pairs={{0,16},{16,0},{32,48},{48,32},{64,80},{80,64},{96,112},{112,96},{1... | collective-permute-start | bytes 393224 | tf_op jit(solution)/shard_map/ppermute | solution.py:212
  7.7 11.1 %collective-permute-start.1 = (bf16[512,128]{1,0:T(8,128)(2,1)S(1)}, bf16[512,128]{1,0:T(8,128)(2,1)S(1)}, u32[]{:S(2)}, u32[]{:S(2)}) collective-permute-start(bf16[512,128]{1,0:T(8,128)(2,1)S(1)} %shard_map.46.refs_1_), channel_id=1, source_target_pairs={{0,496},{16,32},{32,16},{48,64},{64,48},{80,96},{96,80},{112,128},... | collective-permute-start | bytes 393224 | tf_op jit(solution)/shard_map/ppermute | solution.py:211
  18.8 0.0 collective-permute-done.refs_0_
  18.8 2.9 %collective-permute-done.1.refs_2_ = bf16[512,128]{1,0:T(8,128)(2,1)S(1)} collective-permute-done((bf16[512,128]{1,0:T(8,128)(2,1)S(1)}, bf16[512,128]{1,0:T(8,128)(2,1)S(1)}, u32[]{:S(2)}, u32[]{:S(2)}) %collective-permute-start.1) | collective-permute-done | bytes 131104 | tf_op jit(solution)/shard_map/ppermute | solution.py:211
  21.7 0.0 copy-start.1
  21.7 1.6 %copy-done.1 = bf16[32,256,128]{2,1,0:T(8,128)(2,1)S(1)} copy-done((bf16[32,256,128]{2,1,0:T(8,128)(2,1)S(1)}, bf16[32,256,128]{2,1,0:T(8,128)(2,1)}, u32[]{:S(2)}) %copy-start.1) | copy-done | bytes 2097176
  23.3 0.0 copy-start.4
  23.3 0.7 copy-done.4
  24.0 4.8 %shard_map.47 = bf16[256,64,128]{2,1,0:T(8,128)(2,1)S(1)} custom-call(bf16[512,128]{1,0:T(8,128)(2,1)S(1)} %collective-permute-done.refs_0_, bf16[512,128]{1,0:T(8,128)(2,1)S(1)} %shard_map.46.refs_1_, bf16[512,128]{1,0:T(8,128)(2,1)S(1)} %collective-permute-done.1.refs_2_, s32[4,128]{1,0:T(4,128)S(1)} %bitcast.5, bf16[32,256,128]{2,1,0:T(8,128)(2,1)S(1)} %copy-done.1), custom_call_target="tpu_custom_call" | custom-call | tf_op jit(solution)/shard_map/pallas_call | solution.py:149
  28.8 0.0 copy-start
  28.8 2.0 %copy-done = bf16[256,64,128]{2,1,0:T(8,128)(2,1)} copy-done((bf16[256,64,128]{2,1,0:T(8,128)(2,1)}, bf16[256,64,128]{2,1,0:T(8,128)(2,1)S(1)}, u32[]{:S(2)}) %copy-start) | copy-done | bytes 4194328
  30.8 8.5 %all-to-all-start = ((bf16[16,16,64,128]{3,2,1,0:T(8,128)(2,1)}), bf16[16,16,64,128]{3,2,1,0:T(8,128)(2,1)}, u32[]{:S(2)}, u32[]{:S(2)}) async-start(bf16[16,16,64,128]{3,2,1,0:T(8,128)(2,1)} %bitcast.3), calls=%async_computation | async-start | bytes 8388608 | tf_op jit(solution)/shard_map/all_to_all | solution.py:215
  39.3 10.7 %select_convert_fusion.table_ref = bf16[1024,512]{1,0:T(8,128)(2,1)S(1)} fusion(s32[1024]{0:T(1024)S(1)} %get-tuple-element.5, s32[1024]{0:T(1024)S(1)} %get-tuple-element.8, s32[1024]{0:T(1024)S(1)} %get-tuple-element.6, s32[1024]{0:T(1024)S(1)} %get-tuple-element.7, pred[1024]{0:T(1024)(128)(4,1)S(1)} %get-tuple-element.9, ...), kind=kLoop, calls=%fused_computation.20 | loop fusion | flops 24117248 | bytes 1067008 | tf_op jit(solution)/shard_map/convert_element_type | solution.py:27
  50.0 40.3 %all-to-all-done.block_ref = bf16[16,16,64,128]{3,2,1,0:T(8,128)(2,1)} async-done(((bf16[16,16,64,128]{3,2,1,0:T(8,128)(2,1)}), bf16[16,16,64,128]{3,2,1,0:T(8,128)(2,1)}, u32[]{:S(2)}, u32[]{:S(2)}) %all-to-all-start) | async-done | bytes 4194336 | tf_op jit(solution)/shard_map/all_to_all | solution.py:215
  90.4 6.1 %shard_map.48 = bf16[16,128,1024]{2,1,0:T(8,128)(2,1)} custom-call(bf16[16,16,64,128]{3,2,1,0:T(8,128)(2,1)} %all-to-all-done.block_ref, bf16[1024,512]{1,0:T(8,128)(2,1)S(1)} %select_convert_fusion.table_ref), custom_call_target="tpu_custom_call" | custom-call | tf_op jit(solution)/shard_map/pallas_call | solution.py:190
  (3 shorter events, 0.0 us)
Async XLA Ops:
  0.0 0.9 copy-start.2
  0.9 0.9 copy-start.3
  3.8 15.1 %collective-permute-start = (bf16[512,128]{1,0:T(8,128)(2,1)S(1)}, bf16[512,128]{1,0:T(8,128)(2,1)S(1)}, u32[]{:S(2)}, u32[]{:S(2)}) collective-permute-start(bf16[512,128]{1,0:T(8,128)(2,1)S(1)} %shard_map.46.refs_1_), channel_id=1, source_target_pairs={{0,16},{16,0},{32,48},{48,32},{64,80},{80,64},{96,112},{112,96},{1... | collective-permute-start | bytes 393224 | tf_op jit(solution)/shard_map/ppermute | solution.py:212
  7.7 14.0 %collective-permute-start.1 = (bf16[512,128]{1,0:T(8,128)(2,1)S(1)}, bf16[512,128]{1,0:T(8,128)(2,1)S(1)}, u32[]{:S(2)}, u32[]{:S(2)}) collective-permute-start(bf16[512,128]{1,0:T(8,128)(2,1)S(1)} %shard_map.46.refs_1_), channel_id=1, source_target_pairs={{0,496},{16,32},{32,16},{48,64},{64,48},{80,96},{96,80},{112,128},... | collective-permute-start | bytes 393224 | tf_op jit(solution)/shard_map/ppermute | solution.py:211
  21.7 1.6 %copy-start.1 = (bf16[32,256,128]{2,1,0:T(8,128)(2,1)S(1)}, bf16[32,256,128]{2,1,0:T(8,128)(2,1)}, u32[]{:S(2)}) copy-start(bf16[32,256,128]{2,1,0:T(8,128)(2,1)} %refs_4_.1) | copy-start | bytes 6291460
  23.3 0.7 copy-start.4
  28.8 2.0 %copy-start = (bf16[256,64,128]{2,1,0:T(8,128)(2,1)}, bf16[256,64,128]{2,1,0:T(8,128)(2,1)S(1)}, u32[]{:S(2)}) copy-start(bf16[256,64,128]{2,1,0:T(8,128)(2,1)S(1)} %shard_map.47) | copy-start | bytes 12582916
  30.8 59.6 %all-to-all-start = ((bf16[16,16,64,128]{3,2,1,0:T(8,128)(2,1)}), bf16[16,16,64,128]{3,2,1,0:T(8,128)(2,1)}, u32[]{:S(2)}, u32[]{:S(2)}) async-start(bf16[16,16,64,128]{3,2,1,0:T(8,128)(2,1)} %bitcast.3), calls=%async_computation | async-start | bytes 8388608 | tf_op jit(solution)/shard_map/all_to_all | solution.py:215

commit v3 on v2

v3 whole, which is shorter than its diff:
```python
import math

import jax
import jax.numpy as jnp
from jax import lax
from jax.experimental import pallas as pl
from jax.experimental.pallas import tpu as pltpu
from jax.sharding import PartitionSpec as P

BF16 = jnp.bfloat16
F32 = jnp.float32
LANES = 128
SUBS = 8
ROWS16 = 16
MIB = 2**20
PIECES = 4


def half_table(modes):
    angles = 2 * modes
    row = lax.broadcasted_iota(jnp.int32, (2 * modes, modes), 0)
    angle = lax.broadcasted_iota(jnp.int32, (2 * modes, modes), 1)
    parity = row // modes
    rest = row % modes
    order = (rest // 2) * 2 + parity
    phase = (order * angle % angles).astype(F32) * (2.0 * math.pi / angles)
    weight = jnp.where(order == 0, 1.0, 2.0).astype(F32) / math.sqrt(2.0 * modes)
    return jnp.where(rest % 2 == 0, weight * jnp.cos(phase), -weight * jnp.sin(phase)).astype(BF16)


def one_hot_order(index, owner, hot):
    width = hot.shape[0]
    index = index - owner * width
    spot = lax.broadcasted_iota(jnp.int32, (SUBS, LANES), 0)
    for q in range(SUBS):
        low = index[q : q + 1, :] - spot
        for first in range(0, width, ROWS16):
            pair = [jnp.where(low == first + shift, 1.0, 0.0) for shift in (0, SUBS)]
            hot[first : first + ROWS16, q * LANES : (q + 1) * LANES] = jnp.concatenate(pair, axis=0).astype(BF16)


def box_rows(charges, hot, rows):
    modes, parts, width = charges.shape
    count = modes * parts
    moved = jnp.dot(charges[...].reshape(count, width), hot[...], preferred_element_type=F32)
    for q in range(SUBS):
        rows[pl.ds(q, count, stride=SUBS), :] = moved[:, q * LANES : (q + 1) * LANES]
    return rows[...].astype(BF16)


def owners():
    tile = lax.axis_index("tile")
    toward = 1 - 2 * lax.rem(tile, 2)
    return tile + toward, tile, tile - toward


def prepare_kernel(
    boxes,
    charges_hbm,
    skel_hbm,
    lists_hbm,
    proxy_hbm,
    order_ref,
    own_ref,
    pick_ref,
    proxy_ref,
    charges,
    skel,
    lists,
    hot,
    rows,
    sems,
):
    slots = skel.shape[1]
    count, tiles = lists.shape
    cols = count * tiles
    groups = LANES // boxes
    total = skel_hbm.shape[1] // boxes
    places = [jnp.clip(owner, 0, total - 1) for owner in owners()]
    copies = []
    for o, place in enumerate(places):
        column = pl.multiple_of(place // groups * LANES, LANES)
        copies.append(pltpu.make_async_copy(skel_hbm.at[:, pl.ds(column, LANES)], skel.at[o], sems.at[o]))
    copies.append(pltpu.make_async_copy(charges_hbm, charges, sems.at[3]))
    copies.append(pltpu.make_async_copy(lists_hbm, lists, sems.at[4]))
    for copy in copies:
        copy.start()
    modes = proxy_hbm.shape[0]
    per = modes // PIECES
    fetches = []
    for k in range(PIECES):
        span = pl.ds(k * per, per)
        fetches.append(pltpu.make_async_copy(proxy_hbm.at[span], proxy_ref.at[span], sems.at[5 + k]))
        fetches[-1].start()
    pick_ref[...] = jnp.zeros_like(pick_ref)
    for copy in copies:
        copy.wait()
    lane = lax.broadcasted_iota(jnp.int32, (SUBS, LANES), 1)
    for o in (1, 0, 2):
        index = jnp.zeros((SUBS, LANES), jnp.int32)
        for u in range(slots // SUBS):
            shift = lax.rem(u * boxes - lax.rem(places[o], groups) * boxes + LANES, LANES)
            moved = pltpu.roll(skel[o, u * SUBS : (u + 1) * SUBS, :], shift, 1)
            index = jnp.where(lane // boxes == u, moved, index)
        one_hot_order(index, places[o], hot if o == 1 else order_ref.at[o // 2])
        if o == 1:
            own_ref[...] = box_rows(charges, hot, rows)
    box = lax.broadcasted_iota(jnp.int32, (boxes, tiles), 0)
    for o, owner in enumerate(owners()):
        for l in range(count):
            block = jnp.where(box == lists[l : l + 1, :] - owner * boxes, 1.0, 0.0).astype(BF16)
            for u in range(groups):
                pick_ref[
                    o * LANES + u * boxes : o * LANES + (u + 1) * boxes,
                    u * cols + l * tiles : u * cols + (l + 1) * tiles,
                ] = block
    for fetch in fetches:
        fetch.wait()


def prepare(charges, skel_t, lists, proxy):
    modes, parts, width = charges.shape
    slots = skel_t.shape[0]
    boxes = width // slots
    count, tiles = lists.shape
    rows = modes * parts * SUBS

    def body(*refs):
        prepare_kernel(boxes, *refs)

    held = pl.BlockSpec(memory_space=pltpu.VMEM)
    return pl.pallas_call(
        body,
        out_shape=[
            pltpu.VMEM((2, width, width), BF16),
            pltpu.VMEM((rows, LANES), BF16),
            pltpu.VMEM((3 * LANES, LANES // boxes * count * tiles), BF16),
            pltpu.VMEM(proxy.shape, BF16),
        ],
        in_specs=[pl.BlockSpec(memory_space=pltpu.HBM)] * 4,
        out_specs=[held] * 4,
        scratch_shapes=[
            pltpu.VMEM(charges.shape, BF16),
            pltpu.VMEM((3, slots, LANES), jnp.int32),
            pltpu.VMEM((count, tiles), jnp.int32),
            pltpu.VMEM((width, width), BF16),
            pltpu.VMEM((rows, LANES), F32),
            pltpu.SemaphoreType.DMA((5 + PIECES,)),
        ],
        compiler_params=pltpu.CompilerParams(vmem_limit_bytes=24 * MIB),
    )(*(pltpu.with_memory_space_constraint(x, pltpu.HBM) for x in (charges, skel_t, lists, proxy)))


def field_kernel(groups, tiles, near, own, far, order, pick, proxy, out_hbm, picked, field, rows, sems):
    modes, targets, depth = proxy.shape
    cols = pick.shape[1] // groups
    count = cols // tiles
    source = jnp.concatenate(
        [box_rows(near, order.at[0], rows.at[0]), own[...], box_rows(far, order.at[1], rows.at[1])], axis=1
    )
    for h in range(groups // 2):
        got = jnp.dot(source, pick[:, 2 * h * cols : 2 * (h + 1) * cols], preferred_element_type=F32)
        got = got.reshape(modes, 2, SUBS, 2 * cols)
        for l in range(count):
            low = got[..., l * tiles : (l + 1) * tiles]
            high = got[..., cols + l * tiles : cols + (l + 1) * tiles]
            both = jnp.concatenate([low, high], axis=2).astype(BF16)
            first = l * (groups * SUBS) + h * 2 * SUBS
            for c in range(2):
                picked[:, first : first + 2 * SUBS, c * tiles : (c + 1) * tiles] = both[:, c]
    per = ROWS16 // 2
    half = modes // 2
    writes = []
    for g in range(modes // per):
        parts = []
        for j in range(per):
            m = g // (half // per) + 2 * (g % (half // per) * per + j)
            res = jnp.dot(proxy[m], picked[m], preferred_element_type=F32).astype(BF16)
            parts += [res[:, :tiles], res[:, tiles:]]
        span = slice(g * ROWS16, (g + 1) * ROWS16)
        wide = targets // PIECES
        for k in range(PIECES):
            chunk = slice(k * wide, (k + 1) * wide)
            stack = jnp.stack([part[chunk] for part in parts], axis=0)
            field[chunk, span, :] = jnp.swapaxes(stack, 0, 1)
            copy = pltpu.make_async_copy(
                field.at[chunk, span, :], out_hbm.at[chunk, span, :], sems.at[g * PIECES + k]
            )
            copy.start()
            writes.append(copy)
    for copy in writes:
        copy.wait()


def fields(near, own, far, order, pick, proxy, boxes, tiles):
    modes, targets, depth = proxy.shape
    groups = LANES // boxes

    def body(*refs):
        field_kernel(groups, tiles, *refs)

    held = pl.BlockSpec(memory_space=pltpu.VMEM)
    placed = pl.BlockSpec(memory_space=pltpu.HBM)
    shape = (targets, 2 * modes, tiles)
    return pl.pallas_call(
        body,
        out_shape=pltpu.HBM(shape, BF16),
        in_specs=[held] * 6,
        out_specs=placed,
        scratch_shapes=[
            pltpu.VMEM((modes, depth, 2 * tiles), BF16),
            pltpu.VMEM(shape, BF16),
            pltpu.VMEM((2,) + own.shape, F32),
            pltpu.SemaphoreType.DMA((2 * modes // ROWS16 * PIECES,)),
        ],
        compiler_params=pltpu.CompilerParams(vmem_limit_bytes=32 * MIB),
    )(near, own, far, order, pick, proxy)


def synth_kernel(step, block_hbm, table_hbm, out_hbm, block, table, out, sems):
    peers, targets, rows, tiles = block.shape
    half = rows // 2
    depth = peers * half
    width = table.shape[1]
    chunks = targets // step
    table_copy = pltpu.make_async_copy(table_hbm, table, sems.at[2 * chunks])
    reads = []
    for k in range(chunks):
        span = pl.ds(k * step, step)
        reads.append(pltpu.make_async_copy(block_hbm.at[:, span], block.at[:, span], sems.at[k]))
        reads[-1].start()
        if k == 0:
            table_copy.start()
    table_copy.wait()
    writes = []
    for k in range(chunks):
        reads[k].wait()
        sums = []
        for parity in range(2):
            parts = [
                block[:, k * step + p, parity * half : (parity + 1) * half, :].reshape(depth, tiles)
                for p in range(step)
            ]
            weights = table[parity * depth : (parity + 1) * depth, :]
            sums.append(
                lax.dot_general(
                    jnp.concatenate(parts, axis=1), weights, (((0,), (0,)), ((), ())), preferred_element_type=F32
                )
            )
        even, odd = sums
        span = slice(k * step, (k + 1) * step)
        out[span, :, :width] = (even + odd).astype(BF16).reshape(step, tiles, width)
        out[span, :, width:] = (even - odd).astype(BF16).reshape(step, tiles, width)
        writes.append(pltpu.make_async_copy(out.at[span], out_hbm.at[span], sems.at[chunks + k]))
        writes[-1].start()
    for copy in writes:
        copy.wait()


def synthesis(block, table, step):
    peers, targets, rows, tiles = block.shape
    angles = 2 * table.shape[1]
    shape = (targets, tiles, angles)

    def body(*refs):
        synth_kernel(step, *refs)

    placed = pl.BlockSpec(memory_space=pltpu.HBM)
    return pl.pallas_call(
        body,
        out_shape=pltpu.HBM(shape, BF16),
        in_specs=[placed] * 2,
        out_specs=placed,
        scratch_shapes=[
            pltpu.VMEM(block.shape, BF16),
            pltpu.VMEM(table.shape, BF16),
            pltpu.VMEM(shape, BF16),
            pltpu.SemaphoreType.DMA((2 * targets // step + 1,)),
        ],
        compiler_params=pltpu.CompilerParams(vmem_limit_bytes=40 * MIB),
    )(*(pltpu.with_memory_space_constraint(x, pltpu.HBM) for x in (block, table)))


def shards(charges, proxy, tile_boxes, box_skel):
    modes_here, parts, skel_here = charges.shape
    _, targets, _ = proxy.shape
    tiles_here, _ = tile_boxes.shape
    slots = box_skel.shape[1]
    peers = lax.axis_size("mode")
    groups = lax.axis_size("tile")
    far = lax.ppermute(charges, "tile", [(i, (i - 1 + 2 * (i % 2)) % groups) for i in range(groups)])
    near = lax.ppermute(charges, "tile", [(i, i + 1 - 2 * (i % 2)) for i in range(groups)])
    order, own, pick, proxy = prepare(charges, box_skel.T, tile_boxes.T, proxy)
    field = fields(near, own, far, order, pick, proxy, skel_here // slots, tiles_here)
    field = field.reshape(peers, targets // peers, modes_here * parts, tiles_here)
    block = lax.all_to_all(field, "mode", split_axis=0, concat_axis=0, tiled=True)
    table = half_table(modes_here * peers)
    return synthesis(block, table, 4)


def solution(mesh):
    placed = (P("mode", None, "tile"), P("mode", None, None), P("tile", None), P())
    return jax.shard_map(
        shards, mesh=mesh, in_specs=placed, out_specs=P("mode", "tile", None), check_vma=False
    )
```

time: 96.9 us -> 88.4 us (0.912)
  local copies, waits for them, and re-layouts: 6.09 us -> 0 us
  waiting for transfers between devices: 43.2 us -> 39.7 us
    unnamed x10 -> x0, local copies, waits for them, and re-layouts: 6.09 us -> none
    ppermute x2, waiting for transfers between devices: 2.88 us -> 0.01 us  [the longest x1 0.01 us: shards(): lax.ppermute(charges, 'tile', [(i, i + 1 - 2 * (i % 2)) for i in range(gr...]
  transfers between devices with their start and end apart: 3 -> 3, of which waited for: 2 -> 1; matrix products, arithmetic and copies ran while one was open for 11% -> 13% of each run, Pallas kernels for 0% -> 4%
where the time goes in v3:
time: 88.4 us; the launch traced here: 88.1 us
  waiting for transfers between devices  39.7 us (45%)
  starting transfers between devices  23.3 us (26%)
  Pallas kernels  13.7 us (15%)
  other arithmetic  11.4 us (13%)
    all_to_all x1, waiting for transfers between devices, shards(): lax.all_to_all(field, 'mode', split_axis=0, concat_axis=0, tiled=True)  39.7 us
    convert_element_type x1, other arithmetic, half_table(): jnp.where(rest % 2 == 0, weight * jnp.cos(phase), -weight * jnp.sin(phase))  11.4 us
    ppermute x1, starting transfers between devices, shards(): lax.ppermute(charges, 'tile', [(i, (i - 1 + 2 * (i % 2)) % groups) for i...  11.1 us
    all_to_all x1, starting transfers between devices, shards(): lax.all_to_all(field, 'mode', split_axis=0, concat_axis=0, tiled=True)  8.26 us
    pallas_call x1, Pallas kernels, synthesis(): pl.pallas_call(body, out_shape=pltpu.HBM(shape, BF16), in_specs=[placed]...  5.56 us
    pallas_call x1, Pallas kernels, fields(): pl.pallas_call(body, out_shape=pltpu.HBM(shape, BF16), in_specs=[held] *...  4.84 us
    ppermute x1, starting transfers between devices, shards(): lax.ppermute(charges, 'tile', [(i, i + 1 - 2 * (i % 2)) for i in range(gr...  3.94 us
    pallas_call x1, Pallas kernels, prepare(): pl.pallas_call(body, out_shape=[pltpu.VMEM((2, width, width), BF16), pltp...  3.31 us
  transfers between devices with their start and end apart: 3, of which 1 were waited for; matrix products, arithmetic and copies ran while one was open for 13% of the time, Pallas kernels for 4%

profile of v3, /device:TPU:1, one launch (start us, length us, event | category | flops | bytes accessed | tf_op | source)
XLA Modules:
  0.0 88.1 jit_solution(7740696772276491129)
XLA Ops:
  0.0 3.9 %collective-permute-start = (bf16[32,2,1024]{2,1,0:T(2,128)(2,1)}, bf16[32,2,1024]{2,1,0:T(2,128)(2,1)S(1)}, u32[]{:S(2)}, u32[]{:S(2)}) collective-permute-start(bf16[32,2,1024]{2,1,0:T(2,128)(2,1)} %refs_0_.1), channel_id=1, source_target_pairs={{0,16},{16,0},{32,48},{48,32},{64,80},{80,64},{96,112},{112,96},{1... | collective-permute-start | bytes 393224 | tf_op jit(solution)/shard_map/ppermute | solution.py:292
  3.9 11.1 %collective-permute-start.1 = (bf16[32,2,1024]{2,1,0:T(2,128)(2,1)}, bf16[32,2,1024]{2,1,0:T(2,128)(2,1)S(1)}, u32[]{:S(2)}, u32[]{:S(2)}) collective-permute-start(bf16[32,2,1024]{2,1,0:T(2,128)(2,1)} %refs_0_.1), channel_id=1, source_target_pairs={{0,496},{16,32},{32,16},{48,64},{64,48},{80,96},{96,80},{112,128},... | collective-permute-start | bytes 393224 | tf_op jit(solution)/shard_map/ppermute | solution.py:291
  15.0 3.3 %shard_map.46 = (bf16[2,1024,1024]{2,1,0:T(8,128)(2,1)S(1)}, bf16[512,128]{1,0:T(8,128)(2,1)S(1)}, bf16[384,2048]{1,0:T(8,128)(2,1)S(1)}, bf16[32,256,128]{2,1,0:T(8,128)(2,1)S(1)}) custom-call(bf16[32,2,1024]{2,1,0:T(2,128)(2,1)} %refs_0_.1, s32[32,1024]{1,0:T(8,128)} %bitcast.4, s32[4,128]{1,0:T(4,128)} %bitcast.5, bf16[32,256,128]{2,1,0:T(8,128)(2,1)} %refs_3_.1), custom_call_target="tpu_custom_call" | custom-call | tf_op jit(solution)/shard_map/pallas_call | solution.py:132
  18.4 0.0 collective-permute-done.refs_0_
  18.4 0.0 collective-permute-done.1.refs_2_
  18.4 4.8 %shard_map.47 = bf16[256,64,128]{2,1,0:T(8,128)(2,1)} custom-call(bf16[32,2,1024]{2,1,0:T(2,128)(2,1)S(1)} %collective-permute-done.refs_0_, bf16[512,128]{1,0:T(8,128)(2,1)S(1)} %get-tuple-element.9.refs_1_, bf16[32,2,1024]{2,1,0:T(2,128)(2,1)S(1)} %collective-permute-done.1.refs_2_, bf16[2,1024,1024]{2,1,0:T(8,128)(2,1)S(1)} %get-tuple-element.10.refs_3_, ...), custom_call_target="tpu_custom_call" | custom-call | tf_op jit(solution)/shard_map/pallas_call | solution.py:205
  23.2 8.3 %all-to-all-start = ((bf16[16,16,64,128]{3,2,1,0:T(8,128)(2,1)}), bf16[16,16,64,128]{3,2,1,0:T(8,128)(2,1)}, u32[]{:S(2)}, u32[]{:S(2)}) async-start(bf16[16,16,64,128]{3,2,1,0:T(8,128)(2,1)} %bitcast.3), calls=%async_computation | async-start | bytes 8388608 | tf_op jit(solution)/shard_map/all_to_all | solution.py:296
  31.5 11.4 %select_convert_fusion.refs_1_ = bf16[1024,512]{1,0:T(8,128)(2,1)} fusion(s32[1024]{0:T(1024)S(1)} %get-tuple-element.13, s32[1024]{0:T(1024)S(1)} %get-tuple-element.16, s32[1024]{0:T(1024)S(1)} %get-tuple-element.14, s32[1024]{0:T(1024)S(1)} %get-tuple-element.15, pred[1024]{0:T(1024)(128)(4,1)S(1)} %get-tuple-element.17, ...), kind=kLoop, calls=%fused_computation.20 | loop fusion | flops 24117248 | bytes 1067008 | tf_op jit(solution)/shard_map/convert_element_type | solution.py:28
  42.9 39.7 %all-to-all-done.refs_0_ = bf16[16,16,64,128]{3,2,1,0:T(8,128)(2,1)} async-done(((bf16[16,16,64,128]{3,2,1,0:T(8,128)(2,1)}), bf16[16,16,64,128]{3,2,1,0:T(8,128)(2,1)}, u32[]{:S(2)}, u32[]{:S(2)}) %all-to-all-start) | async-done | bytes 4194336 | tf_op jit(solution)/shard_map/all_to_all | solution.py:296
  82.6 5.6 %shard_map.48 = bf16[16,128,1024]{2,1,0:T(8,128)(2,1)} custom-call(bf16[16,16,64,128]{3,2,1,0:T(8,128)(2,1)} %all-to-all-done.refs_0_, bf16[1024,512]{1,0:T(8,128)(2,1)} %select_convert_fusion.refs_1_), custom_call_target="tpu_custom_call" | custom-call | tf_op jit(solution)/shard_map/pallas_call | solution.py:269
  (3 shorter events, 0.0 us)
Async XLA Ops:
  0.0 18.4 %collective-permute-start = (bf16[32,2,1024]{2,1,0:T(2,128)(2,1)}, bf16[32,2,1024]{2,1,0:T(2,128)(2,1)S(1)}, u32[]{:S(2)}, u32[]{:S(2)}) collective-permute-start(bf16[32,2,1024]{2,1,0:T(2,128)(2,1)} %refs_0_.1), channel_id=1, source_target_pairs={{0,16},{16,0},{32,48},{48,32},{64,80},{80,64},{96,112},{112,96},{1... | collective-permute-start | bytes 393224 | tf_op jit(solution)/shard_map/ppermute | solution.py:292
  3.9 14.4 %collective-permute-start.1 = (bf16[32,2,1024]{2,1,0:T(2,128)(2,1)}, bf16[32,2,1024]{2,1,0:T(2,128)(2,1)S(1)}, u32[]{:S(2)}, u32[]{:S(2)}) collective-permute-start(bf16[32,2,1024]{2,1,0:T(2,128)(2,1)} %refs_0_.1), channel_id=1, source_target_pairs={{0,496},{16,32},{32,16},{48,64},{64,48},{80,96},{96,80},{112,128},... | collective-permute-start | bytes 393224 | tf_op jit(solution)/shard_map/ppermute | solution.py:291
  23.2 59.4 %all-to-all-start = ((bf16[16,16,64,128]{3,2,1,0:T(8,128)(2,1)}), bf16[16,16,64,128]{3,2,1,0:T(8,128)(2,1)}, u32[]{:S(2)}, u32[]{:S(2)}) async-start(bf16[16,16,64,128]{3,2,1,0:T(8,128)(2,1)} %bitcast.3), calls=%async_computation | async-start | bytes 8388608 | tf_op jit(solution)/shard_map/all_to_all | solution.py:296

commit v4 on v3

--- a/solution.py
+++ b/solution.py
@@ -2,6 +2,8 @@
 
 import jax
 import jax.numpy as jnp
+import ml_dtypes
+import numpy as np
 from jax import lax
 from jax.experimental import pallas as pl
 from jax.experimental.pallas import tpu as pltpu
@@ -14,18 +16,18 @@
 ROWS16 = 16
 MIB = 2**20
 PIECES = 4
+STEPS = (2, 2, 4, 4, 2, 2)
 
 
 def half_table(modes):
     angles = 2 * modes
-    row = lax.broadcasted_iota(jnp.int32, (2 * modes, modes), 0)
-    angle = lax.broadcasted_iota(jnp.int32, (2 * modes, modes), 1)
-    parity = row // modes
-    rest = row % modes
-    order = (rest // 2) * 2 + parity
-    phase = (order * angle % angles).astype(F32) * (2.0 * math.pi / angles)
-    weight = jnp.where(order == 0, 1.0, 2.0).astype(F32) / math.sqrt(2.0 * modes)
-    return jnp.where(rest % 2 == 0, weight * jnp.cos(phase), -weight * jnp.sin(phase)).astype(BF16)
+    rest = np.arange(2 * modes) % modes
+    order = (rest // 2) * 2 + np.arange(2 * modes) // modes
+    phase = (order[:, None] * np.arange(modes)[None, :] % angles).astype(np.float32)
+    phase = phase * np.float32(2.0 * math.pi / angles)
+    weight = np.where(order == 0, 1.0, 2.0).astype(np.float32) / np.float32(math.sqrt(2.0 * modes))
+    wave = np.where((rest % 2 == 0)[:, None], np.cos(phase), -np.sin(phase)).astype(np.float32)
+    return jnp.asarray((weight[:, None] * wave).astype(ml_dtypes.bfloat16))
 
 
 def one_hot_order(index, owner, hot):
@@ -52,6 +54,10 @@
     tile = lax.axis_index("tile")
     toward = 1 - 2 * lax.rem(tile, 2)
     return tile + toward, tile, tile - toward
+
+
+def lane_slot(o, u, groups):
+    return (u + groups // 2) % groups if o == 1 else u
 
 
 def prepare_kernel(
@@ -99,9 +105,10 @@
     for o in (1, 0, 2):
         index = jnp.zeros((SUBS, LANES), jnp.int32)
         for u in range(slots // SUBS):
-            shift = lax.rem(u * boxes - lax.rem(places[o], groups) * boxes + LANES, LANES)
+            v = lane_slot(o, u, groups)
+            shift = lax.rem(v * boxes - lax.rem(places[o], groups) * boxes + LANES, LANES)
             moved = pltpu.roll(skel[o, u * SUBS : (u + 1) * SUBS, :], shift, 1)
-            index = jnp.where(lane // boxes == u, moved, index)
+            index = jnp.where(lane // boxes == v, moved, index)
         one_hot_order(index, places[o], hot if o == 1 else order_ref.at[o // 2])
         if o == 1:
             own_ref[...] = box_rows(charges, hot, rows)
@@ -110,10 +117,8 @@
         for l in range(count):
             block = jnp.where(box == lists[l : l + 1, :] - owner * boxes, 1.0, 0.0).astype(BF16)
             for u in range(groups):
-                pick_ref[
-                    o * LANES + u * boxes : o * LANES + (u + 1) * boxes,
-                    u * cols + l * tiles : u * cols + (l + 1) * tiles,
-                ] = block
+                first = o // 2 * LANES + lane_slot(o, u, groups) * boxes
+                pick_ref[first : first + boxes, u * cols + l * tiles : u * cols + (l + 1) * tiles] = block
     for fetch in fetches:
         fetch.wait()
 
@@ -134,7 +139,7 @@
         out_shape=[
             pltpu.VMEM((2, width, width), BF16),
             pltpu.VMEM((rows, LANES), BF16),
-            pltpu.VMEM((3 * LANES, LANES // boxes * count * tiles), BF16),
+            pltpu.VMEM((2 * LANES, LANES // boxes * count * tiles), BF16),
             pltpu.VMEM(proxy.shape, BF16),
         ],
         in_specs=[pl.BlockSpec(memory_space=pltpu.HBM)] * 4,
@@ -151,14 +156,17 @@
     )(*(pltpu.with_memory_space_constraint(x, pltpu.HBM) for x in (charges, skel_t, lists, proxy)))
 
 
-def field_kernel(groups, tiles, near, own, far, order, pick, proxy, out_hbm, picked, field, rows, sems):
+def field_kernel(groups, tiles, near, own, far, order, pick, proxy, field, picked, rows):
     modes, targets, depth = proxy.shape
     cols = pick.shape[1] // groups
     count = cols // tiles
-    source = jnp.concatenate(
-        [box_rows(near, order.at[0], rows.at[0]), own[...], box_rows(far, order.at[1], rows.at[1])], axis=1
-    )
+    first_rows = box_rows(near, order.at[0], rows.at[0])
+    last_rows = box_rows(far, order.at[1], rows.at[1])
+    own_rows = own[...]
+    low_half = lax.broadcasted_iota(jnp.int32, own_rows.shape, 1) < LANES // 2
     for h in range(groups // 2):
+        mixed = jnp.where(low_half, first_rows, own_rows) if h == 0 else jnp.where(low_half, own_rows, first_rows)
+        source = jnp.concatenate([mixed, last_rows], axis=1)
         got = jnp.dot(source, pick[:, 2 * h * cols : 2 * (h + 1) * cols], preferred_element_type=F32)
         got = got.reshape(modes, 2, SUBS, 2 * cols)
         for l in range(count):
@@ -170,7 +178,6 @@
                 picked[:, first : first + 2 * SUBS, c * tiles : (c + 1) * tiles] = both[:, c]
     per = ROWS16 // 2
     half = modes // 2
-    writes = []
     for g in range(modes // per):
         parts = []
         for j in range(per):
@@ -183,13 +190,6 @@
             chunk = slice(k * wide, (k + 1) * wide)
             stack = jnp.stack([part[chunk] for part in parts], axis=0)
             field[chunk, span, :] = jnp.swapaxes(stack, 0, 1)
-            copy = pltpu.make_async_copy(
-                field.at[chunk, span, :], out_hbm.at[chunk, span, :], sems.at[g * PIECES + k]
-            )
-            copy.start()
-            writes.append(copy)
-    for copy in writes:
-        copy.wait()
 
 
 def fields(near, own, far, order, pick, proxy, boxes, tiles):
@@ -200,46 +200,31 @@
         field_kernel(groups, tiles, *refs)
 
     held = pl.BlockSpec(memory_space=pltpu.VMEM)
-    placed = pl.BlockSpec(memory_space=pltpu.HBM)
     shape = (targets, 2 * modes, tiles)
     return pl.pallas_call(
         body,
-        out_shape=pltpu.HBM(shape, BF16),
+        out_shape=pltpu.VMEM(shape, BF16),
         in_specs=[held] * 6,
-        out_specs=placed,
+        out_specs=held,
         scratch_shapes=[
             pltpu.VMEM((modes, depth, 2 * tiles), BF16),
-            pltpu.VMEM(shape, BF16),
             pltpu.VMEM((2,) + own.shape, F32),
-            pltpu.SemaphoreType.DMA((2 * modes // ROWS16 * PIECES,)),
         ],
         compiler_params=pltpu.CompilerParams(vmem_limit_bytes=32 * MIB),
     )(near, own, far, order, pick, proxy)
 
 
-def synth_kernel(step, block_hbm, table_hbm, out_hbm, block, table, out, sems):
+def synth_kernel(spans, block, table, out_hbm, out, sems):
     peers, targets, rows, tiles = block.shape
     half = rows // 2
     depth = peers * half
     width = table.shape[1]
-    chunks = targets // step
-    table_copy = pltpu.make_async_copy(table_hbm, table, sems.at[2 * chunks])
-    reads = []
-    for k in range(chunks):
-        span = pl.ds(k * step, step)
-        reads.append(pltpu.make_async_copy(block_hbm.at[:, span], block.at[:, span], sems.at[k]))
-        reads[-1].start()
-        if k == 0:
-            table_copy.start()
-    table_copy.wait()
     writes = []
-    for k in range(chunks):
-        reads[k].wait()
+    for k, (lo, hi) in enumerate(spans):
         sums = []
         for parity in range(2):
             parts = [
-                block[:, k * step + p, parity * half : (parity + 1) * half, :].reshape(depth, tiles)
-                for p in range(step)
+                block[:, p, parity * half : (parity + 1) * half, :].reshape(depth, tiles) for p in range(lo, hi)
             ]
             weights = table[parity * depth : (parity + 1) * depth, :]
             sums.append(
@@ -248,37 +233,37 @@
                 )
             )
         even, odd = sums
-        span = slice(k * step, (k + 1) * step)
-        out[span, :, :width] = (even + odd).astype(BF16).reshape(step, tiles, width)
-        out[span, :, width:] = (even - odd).astype(BF16).reshape(step, tiles, width)
-        writes.append(pltpu.make_async_copy(out.at[span], out_hbm.at[span], sems.at[chunks + k]))
+        out[lo:hi, :, :width] = (even + odd).astype(BF16).reshape(hi - lo, tiles, width)
+        out[lo:hi, :, width:] = (even - odd).astype(BF16).reshape(hi - lo, tiles, width)
+        writes.append(pltpu.make_async_copy(out.at[lo:hi], out_hbm.at[lo:hi], sems.at[k]))
         writes[-1].start()
     for copy in writes:
         copy.wait()
 
 
-def synthesis(block, table, step):
+def synthesis(block, table, steps):
     peers, targets, rows, tiles = block.shape
     angles = 2 * table.shape[1]
     shape = (targets, tiles, angles)
+    ends = [sum(steps[: k + 1]) for k in range(len(steps))]
+    spans = list(zip([0] + ends[:-1], ends))
 
     def body(*refs):
-        synth_kernel(step, *refs)
+        synth_kernel(spans, *refs)
 
     placed = pl.BlockSpec(memory_space=pltpu.HBM)
     return pl.pallas_call(
         body,
         out_shape=pltpu.HBM(shape, BF16),
-        in_specs=[placed] * 2,
+        in_specs=[pl.BlockSpec(memory_space=pltpu.VMEM)] * 2,
         out_specs=placed,
         scratch_shapes=[
-            pltpu.VMEM(block.shape, BF16),
-            pltpu.VMEM(table.shape, BF16),
             pltpu.VMEM(shape, BF16),
-            pltpu.SemaphoreType.DMA((2 * targets // step + 1,)),
-        ],
-        compiler_params=pltpu.CompilerParams(vmem_limit_bytes=40 * MIB),
-    )(*(pltpu.with_memory_space_constraint(x, pltpu.HBM) for x in (block, table)))
+            pltpu.SemaphoreType.DMA((len(spans),)),
+        ],
+        compiler_params=pltpu.CompilerParams(vmem_limit_bytes=16 * MIB),
+        cost_estimate=pl.CostEstimate(flops=2**32, bytes_accessed=2**24, transcendentals=0),
+    )(pltpu.with_memory_space_constraint(block, pltpu.VMEM), table)
 
 
 def shards(charges, proxy, tile_boxes, box_skel):
@@ -295,7 +280,7 @@
     field = field.reshape(peers, targets // peers, modes_here * parts, tiles_here)
     block = lax.all_to_all(field, "mode", split_axis=0, concat_axis=0, tiled=True)
     table = half_table(modes_here * peers)
-    return synthesis(block, table, 4)
+    return synthesis(block, table, STEPS)
 
 
 def solution(mesh):

time: 88.4 us -> 84.1 us (0.951)
  blocking collectives: 0 us -> 58.8 us
  waiting for transfers between devices: 39.7 us -> 0.01 us
  other arithmetic: 11.4 us -> 0 us
  starting transfers between devices: 23.3 us -> 15 us
  Pallas kernels: 13.7 us -> 10 us
    all_to_all x0 -> x1, blocking collectives: none -> 58.8 us  [shards(): lax.all_to_all(field, 'mode', split_axis=0, concat_axis=0, tiled=True)]
    all_to_all x1 -> x0, waiting for transfers between devices: 39.7 us -> none  [shards(): lax.all_to_all(field, 'mode', split_axis=0, concat_axis=0, tiled=True)]
    convert_element_type x1 -> x0, other arithmetic: 11.4 us -> none  [half_table(): jnp.where(rest % 2 == 0, weight * jnp.cos(phase), -weight * jnp.sin(phase))]
    all_to_all x1 -> x0, starting transfers between devices: 8.26 us -> none  [shards(): lax.all_to_all(field, 'mode', split_axis=0, concat_axis=0, tiled=True)]
    pallas_call x2, Pallas kernels: 10.4 us -> 6.73 us  [the longest x1 3.51 us: fields(): pl.pallas_call(body, out_shape=pltpu.VMEM(shape, BF16), in_specs=[held] *...]
  transfers between devices with their start and end apart: 3 -> 2, of which waited for: 1 -> 0; matrix products, arithmetic and copies ran while one was open for 13% -> 0% of each run, Pallas kernels for 4% -> 4%
where the time goes in v4:
time: 84.1 us; the launch traced here: 83.9 us
  blocking collectives  58.8 us (70%)
  starting transfers between devices  15 us (18%)
  Pallas kernels  10 us (12%)
    all_to_all x1, blocking collectives, shards(): lax.all_to_all(field, 'mode', split_axis=0, concat_axis=0, tiled=True)  58.8 us
    ppermute x1, starting transfers between devices, shards(): lax.ppermute(charges, 'tile', [(i, (i - 1 + 2 * (i % 2)) % groups) for i...  11.1 us
    ppermute x1, starting transfers between devices, shards(): lax.ppermute(charges, 'tile', [(i, i + 1 - 2 * (i % 2)) for i in range(gr...  3.94 us
    pallas_call x1, Pallas kernels, fields(): pl.pallas_call(body, out_shape=pltpu.VMEM(shape, BF16), in_specs=[held] *...  3.51 us
    pallas_call x1, Pallas kernels, prepare(): pl.pallas_call(body, out_shape=[pltpu.VMEM((2, width, width), BF16), pltp...  3.28 us
    pallas_call x1, Pallas kernels, synthesis(): pl.pallas_call(body, out_shape=pltpu.HBM(shape, BF16), in_specs=[pl.Block...  3.22 us
  transfers between devices with their start and end apart: 2, of which 0 were waited for; matrix products, arithmetic and copies ran while one was open for 0% of the time, Pallas kernels for 4%

profile of v4, /device:TPU:1, one launch (start us, length us, event | category | flops | bytes accessed | tf_op | source)
XLA Modules:
  0.0 83.9 jit_solution(5733377763888083686)
XLA Ops:
  0.0 3.9 %collective-permute-start = (bf16[32,2,1024]{2,1,0:T(2,128)(2,1)}, bf16[32,2,1024]{2,1,0:T(2,128)(2,1)S(1)}, u32[]{:S(2)}, u32[]{:S(2)}) collective-permute-start(bf16[32,2,1024]{2,1,0:T(2,128)(2,1)} %refs_0_.1), channel_id=1, source_target_pairs={{0,16},{16,0},{32,48},{48,32},{64,80},{80,64},{96,112},{112,96},{1... | collective-permute-start | bytes 393224 | tf_op jit(solution)/shard_map/ppermute | solution.py:277
  3.9 11.1 %collective-permute-start.1 = (bf16[32,2,1024]{2,1,0:T(2,128)(2,1)}, bf16[32,2,1024]{2,1,0:T(2,128)(2,1)S(1)}, u32[]{:S(2)}, u32[]{:S(2)}) collective-permute-start(bf16[32,2,1024]{2,1,0:T(2,128)(2,1)} %refs_0_.1), channel_id=1, source_target_pairs={{0,496},{16,32},{32,16},{48,64},{64,48},{80,96},{96,80},{112,128},... | collective-permute-start | bytes 393224 | tf_op jit(solution)/shard_map/ppermute | solution.py:276
  15.0 3.3 %shard_map.55 = (bf16[2,1024,1024]{2,1,0:T(8,128)(2,1)S(1)}, bf16[512,128]{1,0:T(8,128)(2,1)S(1)}, bf16[256,2048]{1,0:T(8,128)(2,1)S(1)}, bf16[32,256,128]{2,1,0:T(8,128)(2,1)S(1)}) custom-call(bf16[32,2,1024]{2,1,0:T(2,128)(2,1)} %refs_0_.1, s32[32,1024]{1,0:T(8,128)} %bitcast.4, s32[4,128]{1,0:T(4,128)} %bitcast.5, bf16[32,256,128]{2,1,0:T(8,128)(2,1)} %refs_3_.1), custom_call_target="tpu_custom_call" | custom-call | tf_op jit(solution)/shard_map/pallas_call | solution.py:137
  18.3 0.0 collective-permute-done.refs_0_
  18.3 0.0 collective-permute-done.1.refs_2_
  18.4 3.5 %shard_map.56 = bf16[256,64,128]{2,1,0:T(8,128)(2,1)S(1)} custom-call(bf16[32,2,1024]{2,1,0:T(2,128)(2,1)S(1)} %collective-permute-done.refs_0_, bf16[512,128]{1,0:T(8,128)(2,1)S(1)} %get-tuple-element.9.refs_1_, bf16[32,2,1024]{2,1,0:T(2,128)(2,1)S(1)} %collective-permute-done.1.refs_2_, bf16[2,1024,1024]{2,1,0:T(8,128)(2,1)S(1)} %get-tuple-element.10.refs_3_, ...), custom_call_target="tpu_custom_call" | custom-call | tf_op jit(solution)/shard_map/pallas_call | solution.py:204
  21.9 0.0 copy-start
  21.9 58.8 %all_to_all.5.refs_0_ = bf16[16,16,64,128]{3,2,1,0:T(8,128)(2,1)S(1)} all-to-all(bf16[16,16,64,128]{3,2,1,0:T(8,128)(2,1)S(1)} %bitcast.3), channel_id=1, replica_groups=mesh['tile'=32,'mode'=16] {'mode'}, dimensions={0} | all-to-all | bytes 8388608 | tf_op jit(solution)/shard_map/all_to_all | solution.py:281
  80.7 0.0 copy-done
  80.7 3.2 %shard_map.57 = bf16[16,128,1024]{2,1,0:T(8,128)(2,1)} custom-call(bf16[16,16,64,128]{3,2,1,0:T(8,128)(2,1)S(1)} %all_to_all.5.refs_0_, bf16[1024,512]{1,0:T(8,128)(2,1)S(1)} %copy-done), custom_call_target="tpu_custom_call" | custom-call | flops 4294967296 | bytes 16777216 | tf_op jit(solution)/shard_map/pallas_call | solution.py:255
Async XLA Ops:
  0.0 18.3 %collective-permute-start = (bf16[32,2,1024]{2,1,0:T(2,128)(2,1)}, bf16[32,2,1024]{2,1,0:T(2,128)(2,1)S(1)}, u32[]{:S(2)}, u32[]{:S(2)}) collective-permute-start(bf16[32,2,1024]{2,1,0:T(2,128)(2,1)} %refs_0_.1), channel_id=1, source_target_pairs={{0,16},{16,0},{32,48},{48,32},{64,80},{80,64},{96,112},{112,96},{1... | collective-permute-start | bytes 393224 | tf_op jit(solution)/shard_map/ppermute | solution.py:277
  3.9 14.4 %collective-permute-start.1 = (bf16[32,2,1024]{2,1,0:T(2,128)(2,1)}, bf16[32,2,1024]{2,1,0:T(2,128)(2,1)S(1)}, u32[]{:S(2)}, u32[]{:S(2)}) collective-permute-start(bf16[32,2,1024]{2,1,0:T(2,128)(2,1)} %refs_0_.1), channel_id=1, source_target_pairs={{0,496},{16,32},{32,16},{48,64},{64,48},{80,96},{96,80},{112,128},... | collective-permute-start | bytes 393224 | tf_op jit(solution)/shard_map/ppermute | solution.py:276
  21.9 58.8 %copy-start = (bf16[1024,512]{1,0:T(8,128)(2,1)S(1)}, bf16[1024,512]{1,0:T(8,128)(2,1)}, u32[]{:S(2)}) copy-start(bf16[1024,512]{1,0:T(8,128)(2,1)} %constant.2.clone.refs_1_) | copy-start | bytes 3145732

commit v5 on v4

--- a/solution.py
+++ b/solution.py
@@ -273,7 +273,7 @@
     slots = box_skel.shape[1]
     peers = lax.axis_size("mode")
     groups = lax.axis_size("tile")
-    far = lax.ppermute(charges, "tile", [(i, (i - 1 + 2 * (i % 2)) % groups) for i in range(groups)])
+    far = lax.ppermute(charges, "tile", [(i, i - 1 + 2 * (i % 2)) for i in range(1, groups - 1)])
     near = lax.ppermute(charges, "tile", [(i, i + 1 - 2 * (i % 2)) for i in range(groups)])
     order, own, pick, proxy = prepare(charges, box_skel.T, tile_boxes.T, proxy)
     field = fields(near, own, far, order, pick, proxy, skel_here // slots, tiles_here)

time: 84.1 us -> 77.9 us (0.926)
  the two profiles are of different devices: /device:TPU:1 before, /device:TPU:256 now
where the time goes in v5:
time: 77.9 us; the launch traced here: 77.7 us
  blocking collectives  58.4 us (75%)
  Pallas kernels  10 us (13%)
  starting transfers between devices  5.37 us (7%)
  waiting for transfers between devices  3.89 us (5%)
    all_to_all x1, blocking collectives, shards(): lax.all_to_all(field, 'mode', split_axis=0, concat_axis=0, tiled=True)  58.4 us
    ppermute x1, waiting for transfers between devices, shards(): lax.ppermute(charges, 'tile', [(i, i - 1 + 2 * (i % 2)) for i in range(1,...  3.89 us
    pallas_call x1, Pallas kernels, fields(): pl.pallas_call(body, out_shape=pltpu.VMEM(shape, BF16), in_specs=[held] *...  3.51 us
    ppermute x1, starting transfers between devices, shards(): lax.ppermute(charges, 'tile', [(i, i + 1 - 2 * (i % 2)) for i in range(gr...  3.39 us
    pallas_call x1, Pallas kernels, prepare(): pl.pallas_call(body, out_shape=[pltpu.VMEM((2, width, width), BF16), pltp...  3.28 us
    pallas_call x1, Pallas kernels, synthesis(): pl.pallas_call(body, out_shape=pltpu.HBM(shape, BF16), in_specs=[pl.Block...  3.23 us
    ppermute x1, starting transfers between devices, shards(): lax.ppermute(charges, 'tile', [(i, i - 1 + 2 * (i % 2)) for i in range(1,...  1.99 us
  transfers between devices with their start and end apart: 2, of which 1 were waited for; matrix products, arithmetic and copies ran while one was open for 0% of the time, Pallas kernels for 4%

profile of v5, /device:TPU:256, one launch (start us, length us, event | category | flops | bytes accessed | tf_op | source)
XLA Modules:
  0.0 77.7 jit_solution(3001981561104619846)
XLA Ops:
  0.0 3.4 %collective-permute-start = (bf16[32,2,1024]{2,1,0:T(2,128)(2,1)}, bf16[32,2,1024]{2,1,0:T(2,128)(2,1)S(1)}, u32[]{:S(2)}, u32[]{:S(2)}) collective-permute-start(bf16[32,2,1024]{2,1,0:T(2,128)(2,1)} %refs_0_.1), channel_id=1, source_target_pairs={{0,16},{16,0},{32,48},{48,32},{64,80},{80,64},{96,112},{112,96},{1... | collective-permute-start | bytes 393224 | tf_op jit(solution)/shard_map/ppermute | solution.py:277
  3.4 2.0 %collective-permute-start.1 = (bf16[32,2,1024]{2,1,0:T(2,128)(2,1)}, bf16[32,2,1024]{2,1,0:T(2,128)(2,1)S(1)}, u32[]{:S(2)}, u32[]{:S(2)}) collective-permute-start(bf16[32,2,1024]{2,1,0:T(2,128)(2,1)} %refs_0_.1), channel_id=1, source_target_pairs={{16,32},{32,16},{48,64},{64,48},{80,96},{96,80},{112,128},{128,112... | collective-permute-start | bytes 393224 | tf_op jit(solution)/shard_map/ppermute | solution.py:276
  5.4 3.3 %shard_map.55 = (bf16[2,1024,1024]{2,1,0:T(8,128)(2,1)S(1)}, bf16[512,128]{1,0:T(8,128)(2,1)S(1)}, bf16[256,2048]{1,0:T(8,128)(2,1)S(1)}, bf16[32,256,128]{2,1,0:T(8,128)(2,1)S(1)}) custom-call(bf16[32,2,1024]{2,1,0:T(2,128)(2,1)} %refs_0_.1, s32[32,1024]{1,0:T(8,128)} %bitcast.4, s32[4,128]{1,0:T(4,128)} %bitcast.5, bf16[32,256,128]{2,1,0:T(8,128)(2,1)} %refs_3_.1), custom_call_target="tpu_custom_call" | custom-call | tf_op jit(solution)/shard_map/pallas_call | solution.py:137
  8.7 0.0 collective-permute-done.refs_0_
  8.7 3.9 %collective-permute-done.1.refs_2_ = bf16[32,2,1024]{2,1,0:T(2,128)(2,1)S(1)} collective-permute-done((bf16[32,2,1024]{2,1,0:T(2,128)(2,1)}, bf16[32,2,1024]{2,1,0:T(2,128)(2,1)S(1)}, u32[]{:S(2)}, u32[]{:S(2)}) %collective-permute-start.1) | collective-permute-done | bytes 131104 | tf_op jit(solution)/shard_map/ppermute | solution.py:276
  12.6 3.5 %shard_map.56 = bf16[256,64,128]{2,1,0:T(8,128)(2,1)S(1)} custom-call(bf16[32,2,1024]{2,1,0:T(2,128)(2,1)S(1)} %collective-permute-done.refs_0_, bf16[512,128]{1,0:T(8,128)(2,1)S(1)} %get-tuple-element.9.refs_1_, bf16[32,2,1024]{2,1,0:T(2,128)(2,1)S(1)} %collective-permute-done.1.refs_2_, bf16[2,1024,1024]{2,1,0:T(8,128)(2,1)S(1)} %get-tuple-element.10.refs_3_, ...), custom_call_target="tpu_custom_call" | custom-call | tf_op jit(solution)/shard_map/pallas_call | solution.py:204
  16.1 0.0 copy-start
  16.1 58.4 %all_to_all.5.refs_0_ = bf16[16,16,64,128]{3,2,1,0:T(8,128)(2,1)S(1)} all-to-all(bf16[16,16,64,128]{3,2,1,0:T(8,128)(2,1)S(1)} %bitcast.3), channel_id=1, replica_groups=mesh['tile'=32,'mode'=16] {'mode'}, dimensions={0} | all-to-all | bytes 8388608 | tf_op jit(solution)/shard_map/all_to_all | solution.py:281
  74.5 0.0 copy-done
  74.5 3.2 %shard_map.57 = bf16[16,128,1024]{2,1,0:T(8,128)(2,1)} custom-call(bf16[16,16,64,128]{3,2,1,0:T(8,128)(2,1)S(1)} %all_to_all.5.refs_0_, bf16[1024,512]{1,0:T(8,128)(2,1)S(1)} %copy-done), custom_call_target="tpu_custom_call" | custom-call | flops 4294967296 | bytes 16777216 | tf_op jit(solution)/shard_map/pallas_call | solution.py:255
Async XLA Ops:
  0.0 8.7 %collective-permute-start = (bf16[32,2,1024]{2,1,0:T(2,128)(2,1)}, bf16[32,2,1024]{2,1,0:T(2,128)(2,1)S(1)}, u32[]{:S(2)}, u32[]{:S(2)}) collective-permute-start(bf16[32,2,1024]{2,1,0:T(2,128)(2,1)} %refs_0_.1), channel_id=1, source_target_pairs={{0,16},{16,0},{32,48},{48,32},{64,80},{80,64},{96,112},{112,96},{1... | collective-permute-start | bytes 393224 | tf_op jit(solution)/shard_map/ppermute | solution.py:277
  3.4 9.2 %collective-permute-start.1 = (bf16[32,2,1024]{2,1,0:T(2,128)(2,1)}, bf16[32,2,1024]{2,1,0:T(2,128)(2,1)S(1)}, u32[]{:S(2)}, u32[]{:S(2)}) collective-permute-start(bf16[32,2,1024]{2,1,0:T(2,128)(2,1)} %refs_0_.1), channel_id=1, source_target_pairs={{16,32},{32,16},{48,64},{64,48},{80,96},{96,80},{112,128},{128,112... | collective-permute-start | bytes 393224 | tf_op jit(solution)/shard_map/ppermute | solution.py:276
  16.1 58.4 %copy-start = (bf16[1024,512]{1,0:T(8,128)(2,1)S(1)}, bf16[1024,512]{1,0:T(8,128)(2,1)}, u32[]{:S(2)}) copy-start(bf16[1024,512]{1,0:T(8,128)(2,1)} %constant.2.clone.refs_1_) | copy-start | bytes 3145732

commit v6 on v5

--- a/solution.py
+++ b/solution.py
@@ -16,17 +16,25 @@
 ROWS16 = 16
 MIB = 2**20
 PIECES = 4
-STEPS = (2, 2, 4, 4, 2, 2)
-
-
-def half_table(modes):
+STEPS = (2,) * 8
+
+
+def row_order(modes):
+    return np.concatenate([np.arange(0, modes, 4), np.arange(2, modes, 4), np.arange(1, modes, 2)])
+
+
+def wave_table(modes, peers):
     angles = 2 * modes
-    rest = np.arange(2 * modes) % modes
-    order = (rest // 2) * 2 + np.arange(2 * modes) // modes
+    here = modes // peers
+    local = row_order(here)
+    cuts = [local[: here // 4], local[here // 4 : here // 2], local[here // 2 :]]
+    order = np.concatenate([(np.arange(peers)[:, None] * here + cut).reshape(-1) for cut in cuts])
+    order = np.repeat(order, 2)
     phase = (order[:, None] * np.arange(modes)[None, :] % angles).astype(np.float32)
     phase = phase * np.float32(2.0 * math.pi / angles)
     weight = np.where(order == 0, 1.0, 2.0).astype(np.float32) / np.float32(math.sqrt(2.0 * modes))
-    wave = np.where((rest % 2 == 0)[:, None], np.cos(phase), -np.sin(phase)).astype(np.float32)
+    part = np.arange(2 * modes) % 2
+    wave = np.where((part == 0)[:, None], np.cos(phase), -np.sin(phase)).astype(np.float32)
     return jnp.asarray((weight[:, None] * wave).astype(ml_dtypes.bfloat16))
 
 
@@ -156,12 +164,28 @@
     )(*(pltpu.with_memory_space_constraint(x, pltpu.HBM) for x in (charges, skel_t, lists, proxy)))
 
 
+def near_rows_kernel(near, order, out, rows):
+    out[...] = box_rows(near, order.at[0], rows)
+
+
+def near_rows(near, order, like):
+    held = pl.BlockSpec(memory_space=pltpu.VMEM)
+    return pl.pallas_call(
+        near_rows_kernel,
+        out_shape=pltpu.VMEM(like.shape, BF16),
+        in_specs=[held] * 2,
+        out_specs=held,
+        scratch_shapes=[pltpu.VMEM(like.shape, F32)],
+        compiler_params=pltpu.CompilerParams(vmem_limit_bytes=16 * MIB),
+    )(near, order)
+
+
 def field_kernel(groups, tiles, near, own, far, order, pick, proxy, field, picked, rows):
     modes, targets, depth = proxy.shape
     cols = pick.shape[1] // groups
     count = cols // tiles
-    first_rows = box_rows(near, order.at[0], rows.at[0])
-    last_rows = box_rows(far, order.at[1], rows.at[1])
+    first_rows = near[...]
+    last_rows = box_rows(far, order.at[1], rows)
     own_rows = own[...]
     low_half = lax.broadcasted_iota(jnp.int32, own_rows.shape, 1) < LANES // 2
     for h in range(groups // 2):
@@ -177,11 +201,11 @@
             for c in range(2):
                 picked[:, first : first + 2 * SUBS, c * tiles : (c + 1) * tiles] = both[:, c]
     per = ROWS16 // 2
-    half = modes // 2
+    local = row_order(modes)
     for g in range(modes // per):
         parts = []
         for j in range(per):
-            m = g // (half // per) + 2 * (g % (half // per) * per + j)
+            m = int(local[g * per + j])
             res = jnp.dot(proxy[m], picked[m], preferred_element_type=F32).astype(BF16)
             parts += [res[:, :tiles], res[:, tiles:]]
         span = slice(g * ROWS16, (g + 1) * ROWS16)
@@ -208,7 +232,7 @@
         out_specs=held,
         scratch_shapes=[
             pltpu.VMEM((modes, depth, 2 * tiles), BF16),
-            pltpu.VMEM((2,) + own.shape, F32),
+            pltpu.VMEM(own.shape, F32),
         ],
         compiler_params=pltpu.CompilerParams(vmem_limit_bytes=32 * MIB),
     )(near, own, far, order, pick, proxy)
@@ -216,25 +240,28 @@
 
 def synth_kernel(spans, block, table, out_hbm, out, sems):
     peers, targets, rows, tiles = block.shape
-    half = rows // 2
-    depth = peers * half
     width = table.shape[1]
+    quarter = width // 2
+    cuts = ((0, rows // 4, quarter), (rows // 4, rows // 2, quarter), (rows // 2, rows, width))
     writes = []
     for k, (lo, hi) in enumerate(spans):
         sums = []
-        for parity in range(2):
-            parts = [
-                block[:, p, parity * half : (parity + 1) * half, :].reshape(depth, tiles) for p in range(lo, hi)
-            ]
-            weights = table[parity * depth : (parity + 1) * depth, :]
+        for first, last, columns in cuts:
+            depth = peers * (last - first)
+            parts = [block[:, p, first:last, :].reshape(depth, tiles) for p in range(lo, hi)]
+            weights = table[peers * first : peers * last, :columns]
             sums.append(
                 lax.dot_general(
                     jnp.concatenate(parts, axis=1), weights, (((0,), (0,)), ((), ())), preferred_element_type=F32
                 )
             )
-        even, odd = sums
-        out[lo:hi, :, :width] = (even + odd).astype(BF16).reshape(hi - lo, tiles, width)
-        out[lo:hi, :, width:] = (even - odd).astype(BF16).reshape(hi - lo, tiles, width)
+        fours, twos, odd = sums
+        for s, even in enumerate((fours + twos, fours - twos)):
+            near = odd[:, s * quarter : (s + 1) * quarter]
+            at = slice(s * quarter, (s + 1) * quarter)
+            out[lo:hi, :, at] = (even + near).astype(BF16).reshape(hi - lo, tiles, quarter)
+            at = slice(width + s * quarter, width + (s + 1) * quarter)
+            out[lo:hi, :, at] = (even - near).astype(BF16).reshape(hi - lo, tiles, quarter)
         writes.append(pltpu.make_async_copy(out.at[lo:hi], out_hbm.at[lo:hi], sems.at[k]))
         writes[-1].start()
     for copy in writes:
@@ -276,10 +303,10 @@
     far = lax.ppermute(charges, "tile", [(i, i - 1 + 2 * (i % 2)) for i in range(1, groups - 1)])
     near = lax.ppermute(charges, "tile", [(i, i + 1 - 2 * (i % 2)) for i in range(groups)])
     order, own, pick, proxy = prepare(charges, box_skel.T, tile_boxes.T, proxy)
-    field = fields(near, own, far, order, pick, proxy, skel_here // slots, tiles_here)
+    field = fields(near_rows(near, order, own), own, far, order, pick, proxy, skel_here // slots, tiles_here)
     field = field.reshape(peers, targets // peers, modes_here * parts, tiles_here)
     block = lax.all_to_all(field, "mode", split_axis=0, concat_axis=0, tiled=True)
-    table = half_table(modes_here * peers)
+    table = wave_table(modes_here * peers, peers)
     return synthesis(block, table, STEPS)
 
 

time: 77.9 us -> 77 us (0.988)
  the two profiles are of different devices: /device:TPU:256 before, /device:TPU:384 now
where the time goes in v6:
time: 77 us; the launch traced here: 76.8 us
  blocking collectives  58.4 us (76%)
  Pallas kernels  9.59 us (12%)
  starting transfers between devices  7.48 us (10%)
  waiting for transfers between devices  1.28 us (2%)
    all_to_all x1, blocking collectives, shards(): lax.all_to_all(field, 'mode', split_axis=0, concat_axis=0, tiled=True)  58.4 us
    ppermute x1, starting transfers between devices, shards(): lax.ppermute(charges, 'tile', [(i, i - 1 + 2 * (i % 2)) for i in range(1,...  4.1 us
    ppermute x1, starting transfers between devices, shards(): lax.ppermute(charges, 'tile', [(i, i + 1 - 2 * (i % 2)) for i in range(gr...  3.39 us
    pallas_call x1, Pallas kernels, prepare(): pl.pallas_call(body, out_shape=[pltpu.VMEM((2, width, width), BF16), pltp...  3.28 us
    pallas_call x1, Pallas kernels, fields(): pl.pallas_call(body, out_shape=pltpu.VMEM(shape, BF16), in_specs=[held] *...  3.1 us
    pallas_call x1, Pallas kernels, synthesis(): pl.pallas_call(body, out_shape=pltpu.HBM(shape, BF16), in_specs=[pl.Block...  2.71 us
  transfers between devices with their start and end apart: 2, of which 1 were waited for; matrix products, arithmetic and copies ran while one was open for 0% of the time, Pallas kernels for 5%

profile of v6, /device:TPU:384, one launch (start us, length us, event | category | flops | bytes accessed | tf_op | source)
XLA Modules:
  0.0 76.8 jit_solution(17365915476916132976)
XLA Ops:
  0.0 3.4 %collective-permute-start = (bf16[32,2,1024]{2,1,0:T(2,128)(2,1)}, bf16[32,2,1024]{2,1,0:T(2,128)(2,1)S(1)}, u32[]{:S(2)}, u32[]{:S(2)}) collective-permute-start(bf16[32,2,1024]{2,1,0:T(2,128)(2,1)} %refs_0_.1), channel_id=1, source_target_pairs={{0,16},{16,0},{32,48},{48,32},{64,80},{80,64},{96,112},{112,96},{1... | collective-permute-start | bytes 393224 | tf_op jit(solution)/shard_map/ppermute | solution.py:304
  3.4 4.1 %collective-permute-start.1 = (bf16[32,2,1024]{2,1,0:T(2,128)(2,1)}, bf16[32,2,1024]{2,1,0:T(2,128)(2,1)S(1)}, u32[]{:S(2)}, u32[]{:S(2)}) collective-permute-start(bf16[32,2,1024]{2,1,0:T(2,128)(2,1)} %refs_0_.1), channel_id=1, source_target_pairs={{16,32},{32,16},{48,64},{64,48},{80,96},{96,80},{112,128},{128,112... | collective-permute-start | bytes 393224 | tf_op jit(solution)/shard_map/ppermute | solution.py:303
  7.5 3.3 %shard_map.55 = (bf16[2,1024,1024]{2,1,0:T(8,128)(2,1)S(1)}, bf16[512,128]{1,0:T(8,128)(2,1)S(1)}, bf16[256,2048]{1,0:T(8,128)(2,1)S(1)}, bf16[32,256,128]{2,1,0:T(8,128)(2,1)S(1)}) custom-call(bf16[32,2,1024]{2,1,0:T(2,128)(2,1)} %refs_0_.1, s32[32,1024]{1,0:T(8,128)} %bitcast.4, s32[4,128]{1,0:T(4,128)} %bitcast.5, bf16[32,256,128]{2,1,0:T(8,128)(2,1)} %refs_3_.1), custom_call_target="tpu_custom_call" | custom-call | tf_op jit(solution)/shard_map/pallas_call | solution.py:145
  10.8 0.0 collective-permute-done.near
  10.8 0.5 shard_map.56.refs_0_
  11.3 1.3 %collective-permute-done.1.refs_2_ = bf16[32,2,1024]{2,1,0:T(2,128)(2,1)S(1)} collective-permute-done((bf16[32,2,1024]{2,1,0:T(2,128)(2,1)}, bf16[32,2,1024]{2,1,0:T(2,128)(2,1)S(1)}, u32[]{:S(2)}, u32[]{:S(2)}) %collective-permute-start.1) | collective-permute-done | bytes 131104 | tf_op jit(solution)/shard_map/ppermute | solution.py:303
  12.6 3.1 %shard_map.57 = bf16[256,64,128]{2,1,0:T(8,128)(2,1)S(1)} custom-call(bf16[512,128]{1,0:T(8,128)(2,1)S(1)} %shard_map.56.refs_0_, bf16[512,128]{1,0:T(8,128)(2,1)S(1)} %get-tuple-element.10.refs_1_, bf16[32,2,1024]{2,1,0:T(2,128)(2,1)S(1)} %collective-permute-done.1.refs_2_, bf16[2,1024,1024]{2,1,0:T(8,128)(2,1)S(1)} %get-tuple-element.9.order.refs_3_, ...), custom_call_target="tpu_custom_call" | custom-call | tf_op jit(solution)/shard_map/pallas_call | solution.py:228
  15.7 0.0 copy-start
  15.7 58.4 %all_to_all.5.refs_0_ = bf16[16,16,64,128]{3,2,1,0:T(8,128)(2,1)S(1)} all-to-all(bf16[16,16,64,128]{3,2,1,0:T(8,128)(2,1)S(1)} %bitcast.3), channel_id=1, replica_groups=mesh['tile'=32,'mode'=16] {'mode'}, dimensions={0} | all-to-all | bytes 8388608 | tf_op jit(solution)/shard_map/all_to_all | solution.py:308
  74.1 0.0 copy-done
  74.1 2.7 %shard_map.58 = bf16[16,128,1024]{2,1,0:T(8,128)(2,1)} custom-call(bf16[16,16,64,128]{3,2,1,0:T(8,128)(2,1)S(1)} %all_to_all.5.refs_0_, bf16[1024,512]{1,0:T(8,128)(2,1)S(1)} %copy-done), custom_call_target="tpu_custom_call" | custom-call | flops 4294967296 | bytes 16777216 | tf_op jit(solution)/shard_map/pallas_call | solution.py:282
Async XLA Ops:
  0.0 10.8 %collective-permute-start = (bf16[32,2,1024]{2,1,0:T(2,128)(2,1)}, bf16[32,2,1024]{2,1,0:T(2,128)(2,1)S(1)}, u32[]{:S(2)}, u32[]{:S(2)}) collective-permute-start(bf16[32,2,1024]{2,1,0:T(2,128)(2,1)} %refs_0_.1), channel_id=1, source_target_pairs={{0,16},{16,0},{32,48},{48,32},{64,80},{80,64},{96,112},{112,96},{1... | collective-permute-start | bytes 393224 | tf_op jit(solution)/shard_map/ppermute | solution.py:304
  3.4 9.2 %collective-permute-start.1 = (bf16[32,2,1024]{2,1,0:T(2,128)(2,1)}, bf16[32,2,1024]{2,1,0:T(2,128)(2,1)S(1)}, u32[]{:S(2)}, u32[]{:S(2)}) collective-permute-start(bf16[32,2,1024]{2,1,0:T(2,128)(2,1)} %refs_0_.1), channel_id=1, source_target_pairs={{16,32},{32,16},{48,64},{64,48},{80,96},{96,80},{112,128},{128,112... | collective-permute-start | bytes 393224 | tf_op jit(solution)/shard_map/ppermute | solution.py:303
  15.7 58.4 %copy-start = (bf16[1024,512]{1,0:T(8,128)(2,1)S(1)}, bf16[1024,512]{1,0:T(8,128)(2,1)}, u32[]{:S(2)}) copy-start(bf16[1024,512]{1,0:T(8,128)(2,1)} %constant.2.clone.refs_1_) | copy-start | bytes 3145732

commit v7 on v6

--- a/solution.py
+++ b/solution.py
@@ -164,28 +164,28 @@
     )(*(pltpu.with_memory_space_constraint(x, pltpu.HBM) for x in (charges, skel_t, lists, proxy)))
 
 
-def near_rows_kernel(near, order, out, rows):
-    out[...] = box_rows(near, order.at[0], rows)
-
-
-def near_rows(near, order, like):
+def far_rows_kernel(far, order, out, rows):
+    out[...] = box_rows(far, order.at[1], rows)
+
+
+def far_rows(far, order, like):
     held = pl.BlockSpec(memory_space=pltpu.VMEM)
     return pl.pallas_call(
-        near_rows_kernel,
+        far_rows_kernel,
         out_shape=pltpu.VMEM(like.shape, BF16),
         in_specs=[held] * 2,
         out_specs=held,
         scratch_shapes=[pltpu.VMEM(like.shape, F32)],
         compiler_params=pltpu.CompilerParams(vmem_limit_bytes=16 * MIB),
-    )(near, order)
-
-
-def field_kernel(groups, tiles, near, own, far, order, pick, proxy, field, picked, rows):
+    )(far, order)
+
+
+def field_kernel(groups, tiles, far, own, near, order, pick, proxy, field, picked, rows):
     modes, targets, depth = proxy.shape
     cols = pick.shape[1] // groups
     count = cols // tiles
-    first_rows = near[...]
-    last_rows = box_rows(far, order.at[1], rows)
+    first_rows = box_rows(near, order.at[0], rows)
+    last_rows = far[...]
     own_rows = own[...]
     low_half = lax.broadcasted_iota(jnp.int32, own_rows.shape, 1) < LANES // 2
     for h in range(groups // 2):
@@ -216,7 +216,7 @@
             field[chunk, span, :] = jnp.swapaxes(stack, 0, 1)
 
 
-def fields(near, own, far, order, pick, proxy, boxes, tiles):
+def fields(far, own, near, order, pick, proxy, boxes, tiles):
     modes, targets, depth = proxy.shape
     groups = LANES // boxes
 
@@ -235,7 +235,7 @@
             pltpu.VMEM(own.shape, F32),
         ],
         compiler_params=pltpu.CompilerParams(vmem_limit_bytes=32 * MIB),
-    )(near, own, far, order, pick, proxy)
+    )(far, own, near, order, pick, proxy)
 
 
 def synth_kernel(spans, block, table, out_hbm, out, sems):
@@ -303,7 +303,7 @@
     far = lax.ppermute(charges, "tile", [(i, i - 1 + 2 * (i % 2)) for i in range(1, groups - 1)])
     near = lax.ppermute(charges, "tile", [(i, i + 1 - 2 * (i % 2)) for i in range(groups)])
     order, own, pick, proxy = prepare(charges, box_skel.T, tile_boxes.T, proxy)
-    field = fields(near_rows(near, order, own), own, far, order, pick, proxy, skel_here // slots, tiles_here)
+    field = fields(far_rows(far, order, own), own, near, order, pick, proxy, skel_here // slots, tiles_here)
     field = field.reshape(peers, targets // peers, modes_here * parts, tiles_here)
     block = lax.all_to_all(field, "mode", split_axis=0, concat_axis=0, tiled=True)
     table = wave_table(modes_here * peers, peers)

time: 77 us -> 76.9 us (level)
  the two profiles are of different devices: /device:TPU:384 before, /device:TPU:1 now
where the time goes in v7:
time: 76.9 us; the launch traced here: 75.9 us
  blocking collectives  58.7 us (76%)
  Pallas kernels  9.61 us (12%)
  starting transfers between devices  7.45 us (10%)
    all_to_all x1, blocking collectives, shards(): lax.all_to_all(field, 'mode', split_axis=0, concat_axis=0, tiled=True)  58.7 us
    ppermute x1, starting transfers between devices, shards(): lax.ppermute(charges, 'tile', [(i, i + 1 - 2 * (i % 2)) for i in range(gr...  6.8 us
    pallas_call x1, Pallas kernels, prepare(): pl.pallas_call(body, out_shape=[pltpu.VMEM((2, width, width), BF16), pltp...  3.28 us
    pallas_call x1, Pallas kernels, fields(): pl.pallas_call(body, out_shape=pltpu.VMEM(shape, BF16), in_specs=[held] *...  3.12 us
    pallas_call x1, Pallas kernels, synthesis(): pl.pallas_call(body, out_shape=pltpu.HBM(shape, BF16), in_specs=[pl.Block...  2.71 us
  transfers between devices with their start and end apart: 2, of which 0 were waited for; matrix products, arithmetic and copies ran while one was open for 0% of the time, Pallas kernels for 5%

profile of v7, /device:TPU:1, one launch (start us, length us, event | category | flops | bytes accessed | tf_op | source)
XLA Modules:
  0.0 75.9 jit_solution(9018154238927406570)
XLA Ops:
  0.0 0.7 collective-permute-start
  0.7 6.8 %collective-permute-start.1 = (bf16[32,2,1024]{2,1,0:T(2,128)(2,1)}, bf16[32,2,1024]{2,1,0:T(2,128)(2,1)S(1)}, u32[]{:S(2)}, u32[]{:S(2)}) collective-permute-start(bf16[32,2,1024]{2,1,0:T(2,128)(2,1)} %refs_0_.1), channel_id=1, source_target_pairs={{0,16},{16,0},{32,48},{48,32},{64,80},{80,64},{96,112},{112,96},{1... | collective-permute-start | bytes 393224 | tf_op jit(solution)/shard_map/ppermute | solution.py:304
  7.5 3.3 %shard_map.55 = (bf16[2,1024,1024]{2,1,0:T(8,128)(2,1)S(1)}, bf16[512,128]{1,0:T(8,128)(2,1)S(1)}, bf16[256,2048]{1,0:T(8,128)(2,1)S(1)}, bf16[32,256,128]{2,1,0:T(8,128)(2,1)S(1)}) custom-call(bf16[32,2,1024]{2,1,0:T(2,128)(2,1)} %refs_0_.1, s32[32,1024]{1,0:T(8,128)} %bitcast.4, s32[4,128]{1,0:T(4,128)} %bitcast.5, bf16[32,256,128]{2,1,0:T(8,128)(2,1)} %refs_3_.1), custom_call_target="tpu_custom_call" | custom-call | tf_op jit(solution)/shard_map/pallas_call | solution.py:145
  10.8 0.0 collective-permute-done.far
  10.8 0.5 shard_map.56.refs_0_
  11.3 0.0 collective-permute-done.1.refs_2_
  11.3 3.1 %shard_map.57 = bf16[256,64,128]{2,1,0:T(8,128)(2,1)S(1)} custom-call(bf16[512,128]{1,0:T(8,128)(2,1)S(1)} %shard_map.56.refs_0_, bf16[512,128]{1,0:T(8,128)(2,1)S(1)} %get-tuple-element.10.refs_1_, bf16[32,2,1024]{2,1,0:T(2,128)(2,1)S(1)} %collective-permute-done.1.refs_2_, bf16[2,1024,1024]{2,1,0:T(8,128)(2,1)S(1)} %get-tuple-element.9.order.refs_3_, ...), custom_call_target="tpu_custom_call" | custom-call | tf_op jit(solution)/shard_map/pallas_call | solution.py:228
  14.4 0.0 copy-start
  14.4 58.7 %all_to_all.5.refs_0_ = bf16[16,16,64,128]{3,2,1,0:T(8,128)(2,1)S(1)} all-to-all(bf16[16,16,64,128]{3,2,1,0:T(8,128)(2,1)S(1)} %bitcast.3), channel_id=1, replica_groups=mesh['tile'=32,'mode'=16] {'mode'}, dimensions={0} | all-to-all | bytes 8388608 | tf_op jit(solution)/shard_map/all_to_all | solution.py:308
  73.1 0.0 copy-done
  73.1 2.7 %shard_map.58 = bf16[16,128,1024]{2,1,0:T(8,128)(2,1)} custom-call(bf16[16,16,64,128]{3,2,1,0:T(8,128)(2,1)S(1)} %all_to_all.5.refs_0_, bf16[1024,512]{1,0:T(8,128)(2,1)S(1)} %copy-done), custom_call_target="tpu_custom_call" | custom-call | flops 4294967296 | bytes 16777216 | tf_op jit(solution)/shard_map/pallas_call | solution.py:282
Async XLA Ops:
  0.0 10.8 %collective-permute-start = (bf16[32,2,1024]{2,1,0:T(2,128)(2,1)}, bf16[32,2,1024]{2,1,0:T(2,128)(2,1)S(1)}, u32[]{:S(2)}, u32[]{:S(2)}) collective-permute-start(bf16[32,2,1024]{2,1,0:T(2,128)(2,1)} %refs_0_.1), channel_id=1, source_target_pairs={{16,32},{32,16},{48,64},{64,48},{80,96},{96,80},{112,128},{128,112... | collective-permute-start | bytes 393224 | tf_op jit(solution)/shard_map/ppermute | solution.py:303
  0.7 10.6 %collective-permute-start.1 = (bf16[32,2,1024]{2,1,0:T(2,128)(2,1)}, bf16[32,2,1024]{2,1,0:T(2,128)(2,1)S(1)}, u32[]{:S(2)}, u32[]{:S(2)}) collective-permute-start(bf16[32,2,1024]{2,1,0:T(2,128)(2,1)} %refs_0_.1), channel_id=1, source_target_pairs={{0,16},{16,0},{32,48},{48,32},{64,80},{80,64},{96,112},{112,96},{1... | collective-permute-start | bytes 393224 | tf_op jit(solution)/shard_map/ppermute | solution.py:304
  14.4 58.7 %copy-start = (bf16[1024,512]{1,0:T(8,128)(2,1)S(1)}, bf16[1024,512]{1,0:T(8,128)(2,1)}, u32[]{:S(2)}) copy-start(bf16[1024,512]{1,0:T(8,128)(2,1)} %constant.2.clone.refs_1_) | copy-start | bytes 3145732

commit v8 on v6

--- a/solution.py
+++ b/solution.py
@@ -164,33 +164,33 @@
     )(*(pltpu.with_memory_space_constraint(x, pltpu.HBM) for x in (charges, skel_t, lists, proxy)))
 
 
-def near_rows_kernel(near, order, out, rows):
-    out[...] = box_rows(near, order.at[0], rows)
-
-
-def near_rows(near, order, like):
+def near_rows_kernel(near, order, own, out, rows):
+    first_rows = box_rows(near, order.at[0], rows)
+    own_rows = own[...]
+    low_half = lax.broadcasted_iota(jnp.int32, own_rows.shape, 1) < LANES // 2
+    out[0] = jnp.where(low_half, first_rows, own_rows)
+    out[1] = jnp.where(low_half, own_rows, first_rows)
+
+
+def near_rows(near, order, own):
     held = pl.BlockSpec(memory_space=pltpu.VMEM)
     return pl.pallas_call(
         near_rows_kernel,
-        out_shape=pltpu.VMEM(like.shape, BF16),
-        in_specs=[held] * 2,
+        out_shape=pltpu.VMEM((2,) + own.shape, BF16),
+        in_specs=[held] * 3,
         out_specs=held,
-        scratch_shapes=[pltpu.VMEM(like.shape, F32)],
+        scratch_shapes=[pltpu.VMEM(own.shape, F32)],
         compiler_params=pltpu.CompilerParams(vmem_limit_bytes=16 * MIB),
-    )(near, order)
-
-
-def field_kernel(groups, tiles, near, own, far, order, pick, proxy, field, picked, rows):
+    )(near, order, own)
+
+
+def field_kernel(groups, tiles, mixed, far, order, pick, proxy, field, picked, rows):
     modes, targets, depth = proxy.shape
     cols = pick.shape[1] // groups
     count = cols // tiles
-    first_rows = near[...]
     last_rows = box_rows(far, order.at[1], rows)
-    own_rows = own[...]
-    low_half = lax.broadcasted_iota(jnp.int32, own_rows.shape, 1) < LANES // 2
     for h in range(groups // 2):
-        mixed = jnp.where(low_half, first_rows, own_rows) if h == 0 else jnp.where(low_half, own_rows, first_rows)
-        source = jnp.concatenate([mixed, last_rows], axis=1)
+        source = jnp.concatenate([mixed[h], last_rows], axis=1)
         got = jnp.dot(source, pick[:, 2 * h * cols : 2 * (h + 1) * cols], preferred_element_type=F32)
         got = got.reshape(modes, 2, SUBS, 2 * cols)
         for l in range(count):
@@ -216,7 +216,7 @@
             field[chunk, span, :] = jnp.swapaxes(stack, 0, 1)
 
 
-def fields(near, own, far, order, pick, proxy, boxes, tiles):
+def fields(mixed, far, order, pick, proxy, boxes, tiles):
     modes, targets, depth = proxy.shape
     groups = LANES // boxes
 
@@ -228,14 +228,14 @@
     return pl.pallas_call(
         body,
         out_shape=pltpu.VMEM(shape, BF16),
-        in_specs=[held] * 6,
+        in_specs=[held] * 5,
         out_specs=held,
         scratch_shapes=[
             pltpu.VMEM((modes, depth, 2 * tiles), BF16),
-            pltpu.VMEM(own.shape, F32),
+            pltpu.VMEM(mixed.shape[1:], F32),
         ],
         compiler_params=pltpu.CompilerParams(vmem_limit_bytes=32 * MIB),
-    )(near, own, far, order, pick, proxy)
+    )(mixed, far, order, pick, proxy)
 
 
 def synth_kernel(spans, block, table, out_hbm, out, sems):
@@ -303,7 +303,7 @@
     far = lax.ppermute(charges, "tile", [(i, i - 1 + 2 * (i % 2)) for i in range(1, groups - 1)])
     near = lax.ppermute(charges, "tile", [(i, i + 1 - 2 * (i % 2)) for i in range(groups)])
     order, own, pick, proxy = prepare(charges, box_skel.T, tile_boxes.T, proxy)
-    field = fields(near_rows(near, order, own), own, far, order, pick, proxy, skel_here // slots, tiles_here)
+    field = fields(near_rows(near, order, own), far, order, pick, proxy, skel_here // slots, tiles_here)
     field = field.reshape(peers, targets // peers, modes_here * parts, tiles_here)
     block = lax.all_to_all(field, "mode", split_axis=0, concat_axis=0, tiled=True)
     table = wave_table(modes_here * peers, peers)

time: 77 us -> 77 us (level)
  the two profiles are of different devices: /device:TPU:384 before, /device:TPU:128 now
where the time goes in v8:
time: 77 us; the launch traced here: 76.8 us
  blocking collectives  58.4 us (76%)
  Pallas kernels  9.61 us (12%)
  starting transfers between devices  5.37 us (7%)
  waiting for transfers between devices  3.36 us (4%)
    all_to_all x1, blocking collectives, shards(): lax.all_to_all(field, 'mode', split_axis=0, concat_axis=0, tiled=True)  58.4 us
    ppermute x1, starting transfers between devices, shards(): lax.ppermute(charges, 'tile', [(i, i + 1 - 2 * (i % 2)) for i in range(gr...  3.39 us
    ppermute x1, waiting for transfers between devices, shards(): lax.ppermute(charges, 'tile', [(i, i - 1 + 2 * (i % 2)) for i in range(1,...  3.36 us
    pallas_call x1, Pallas kernels, prepare(): pl.pallas_call(body, out_shape=[pltpu.VMEM((2, width, width), BF16), pltp...  3.28 us
    pallas_call x1, Pallas kernels, fields(): pl.pallas_call(body, out_shape=pltpu.VMEM(shape, BF16), in_specs=[held] *...  3.1 us
    pallas_call x1, Pallas kernels, synthesis(): pl.pallas_call(body, out_shape=pltpu.HBM(shape, BF16), in_specs=[pl.Block...  2.71 us
    ppermute x1, starting transfers between devices, shards(): lax.ppermute(charges, 'tile', [(i, i - 1 + 2 * (i % 2)) for i in range(1,...  1.99 us
  transfers between devices with their start and end apart: 2, of which 1 were waited for; matrix products, arithmetic and copies ran while one was open for 0% of the time, Pallas kernels for 5%

profile of v8, /device:TPU:128, one launch (start us, length us, event | category | flops | bytes accessed | tf_op | source)
XLA Modules:
  0.0 76.8 jit_solution(2652952454686001504)
XLA Ops:
  0.0 3.4 %collective-permute-start = (bf16[32,2,1024]{2,1,0:T(2,128)(2,1)}, bf16[32,2,1024]{2,1,0:T(2,128)(2,1)S(1)}, u32[]{:S(2)}, u32[]{:S(2)}) collective-permute-start(bf16[32,2,1024]{2,1,0:T(2,128)(2,1)} %refs_0_.1), channel_id=1, source_target_pairs={{0,16},{16,0},{32,48},{48,32},{64,80},{80,64},{96,112},{112,96},{1... | collective-permute-start | bytes 393224 | tf_op jit(solution)/shard_map/ppermute | solution.py:304
  3.4 2.0 %collective-permute-start.1 = (bf16[32,2,1024]{2,1,0:T(2,128)(2,1)}, bf16[32,2,1024]{2,1,0:T(2,128)(2,1)S(1)}, u32[]{:S(2)}, u32[]{:S(2)}) collective-permute-start(bf16[32,2,1024]{2,1,0:T(2,128)(2,1)} %refs_0_.1), channel_id=1, source_target_pairs={{16,32},{32,16},{48,64},{64,48},{80,96},{96,80},{112,128},{128,112... | collective-permute-start | bytes 393224 | tf_op jit(solution)/shard_map/ppermute | solution.py:303
  5.4 3.3 %shard_map.55 = (bf16[2,1024,1024]{2,1,0:T(8,128)(2,1)S(1)}, bf16[512,128]{1,0:T(8,128)(2,1)S(1)}, bf16[256,2048]{1,0:T(8,128)(2,1)S(1)}, bf16[32,256,128]{2,1,0:T(8,128)(2,1)S(1)}) custom-call(bf16[32,2,1024]{2,1,0:T(2,128)(2,1)} %refs_0_.1, s32[32,1024]{1,0:T(8,128)} %bitcast.4, s32[4,128]{1,0:T(4,128)} %bitcast.5, bf16[32,256,128]{2,1,0:T(8,128)(2,1)} %refs_3_.1), custom_call_target="tpu_custom_call" | custom-call | tf_op jit(solution)/shard_map/pallas_call | solution.py:145
  8.7 0.0 collective-permute-done.near
  8.7 0.5 shard_map.56.refs_0_
  9.2 3.4 %collective-permute-done.1.refs_1_ = bf16[32,2,1024]{2,1,0:T(2,128)(2,1)S(1)} collective-permute-done((bf16[32,2,1024]{2,1,0:T(2,128)(2,1)}, bf16[32,2,1024]{2,1,0:T(2,128)(2,1)S(1)}, u32[]{:S(2)}, u32[]{:S(2)}) %collective-permute-start.1) | collective-permute-done | bytes 131104 | tf_op jit(solution)/shard_map/ppermute | solution.py:303
  12.6 3.1 %shard_map.57 = bf16[256,64,128]{2,1,0:T(8,128)(2,1)S(1)} custom-call(bf16[2,512,128]{2,1,0:T(8,128)(2,1)S(1)} %shard_map.56.refs_0_, bf16[32,2,1024]{2,1,0:T(2,128)(2,1)S(1)} %collective-permute-done.1.refs_1_, bf16[2,1024,1024]{2,1,0:T(8,128)(2,1)S(1)} %get-tuple-element.9.order.refs_2_, bf16[256,2048]{1,0:T(8,128)(2,1)S(1)} %get-tuple-element.11.refs_3_, ...), custom_call_target="tpu_custom_call" | custom-call | tf_op jit(solution)/shard_map/pallas_call | solution.py:228
  15.7 0.0 copy-start
  15.7 58.4 %all_to_all.5.refs_0_ = bf16[16,16,64,128]{3,2,1,0:T(8,128)(2,1)S(1)} all-to-all(bf16[16,16,64,128]{3,2,1,0:T(8,128)(2,1)S(1)} %bitcast.3), channel_id=1, replica_groups=mesh['tile'=32,'mode'=16] {'mode'}, dimensions={0} | all-to-all | bytes 8388608 | tf_op jit(solution)/shard_map/all_to_all | solution.py:308
  74.1 0.0 copy-done
  74.1 2.7 %shard_map.58 = bf16[16,128,1024]{2,1,0:T(8,128)(2,1)} custom-call(bf16[16,16,64,128]{3,2,1,0:T(8,128)(2,1)S(1)} %all_to_all.5.refs_0_, bf16[1024,512]{1,0:T(8,128)(2,1)S(1)} %copy-done), custom_call_target="tpu_custom_call" | custom-call | flops 4294967296 | bytes 16777216 | tf_op jit(solution)/shard_map/pallas_call | solution.py:282
Async XLA Ops:
  0.0 8.7 %collective-permute-start = (bf16[32,2,1024]{2,1,0:T(2,128)(2,1)}, bf16[32,2,1024]{2,1,0:T(2,128)(2,1)S(1)}, u32[]{:S(2)}, u32[]{:S(2)}) collective-permute-start(bf16[32,2,1024]{2,1,0:T(2,128)(2,1)} %refs_0_.1), channel_id=1, source_target_pairs={{0,16},{16,0},{32,48},{48,32},{64,80},{80,64},{96,112},{112,96},{1... | collective-permute-start | bytes 393224 | tf_op jit(solution)/shard_map/ppermute | solution.py:304
  3.4 9.2 %collective-permute-start.1 = (bf16[32,2,1024]{2,1,0:T(2,128)(2,1)}, bf16[32,2,1024]{2,1,0:T(2,128)(2,1)S(1)}, u32[]{:S(2)}, u32[]{:S(2)}) collective-permute-start(bf16[32,2,1024]{2,1,0:T(2,128)(2,1)} %refs_0_.1), channel_id=1, source_target_pairs={{16,32},{32,16},{48,64},{64,48},{80,96},{96,80},{112,128},{128,112... | collective-permute-start | bytes 393224 | tf_op jit(solution)/shard_map/ppermute | solution.py:303
  15.7 58.4 %copy-start = (bf16[1024,512]{1,0:T(8,128)(2,1)S(1)}, bf16[1024,512]{1,0:T(8,128)(2,1)}, u32[]{:S(2)}) copy-start(bf16[1024,512]{1,0:T(8,128)(2,1)} %constant.2.clone.refs_1_) | copy-start | bytes 3145732
